TPU v7x, 128 devices: a whole 4x4x4 slice. The times are simulated.
128 devices in a mesh: prow: 8 (over x, core), pcol: 16 (over y, z).
Axes of the slice: x: 4, y: 4, z: 4, core: 2. Of those that a mesh axis runs over, the one named last changes fastest.
Arguments:
- matrix: float32 [16384, 16384], P('prow', 'pcol'), may hold values from -1 to 14, as said below
Outputs:
- factor: float32 [16384, 16384], P('prow', 'pcol')
Inputs may be any that keep to these rules, and one draw needn't show every extreme that they name: In natural order the matrix is symmetric positive definite.
All inputs are finite; a program needn't handle non-finite values.
Results may differ from a plain program's by a relative error of at most 0.0001.
Values sent between devices are 32-bit elements; how exact they have to be, the bound alone decides.
A program may use at most 128 MiB of HBM per device.

v0:
```python
import jax
import jax.numpy as jnp
from jax import lax
from jax.sharding import PartitionSpec as P

NB = 256
STEPS = 4


HIGHEST_PRECISION = lax.Precision.HIGHEST


def spread(block, axis, owner):
    block = jnp.where(lax.axis_index(axis) == owner, block, jnp.zeros_like(block))
    return lax.psum(block, axis)


def factor_rows(column, corner, block):
    nprow = lax.axis_size("prow")
    myrow = lax.axis_index("prow")
    triangle = jnp.linalg.cholesky(corner)
    solved = jax.scipy.linalg.solve_triangular(triangle, column.T, lower=True).T
    blocks = column.shape[0] // NB
    global_block = jnp.arange(column.shape[0]) // NB * nprow + myrow
    stacked = jnp.tile(triangle, (blocks, 1))
    result = jnp.where((global_block > block)[:, None], solved, 0.0)
    return jnp.where((global_block == block)[:, None], stacked, result)


def factor_panel(matrix, block):
    nprow = lax.axis_size("prow")
    npcol = lax.axis_size("pcol")
    myrow = lax.axis_index("prow")
    mycol = lax.axis_index("pcol")
    rows, cols = matrix.shape
    at_column = block // npcol * NB
    at_row = block // nprow * NB
    column = matrix[:, at_column : at_column + NB]
    corner = spread(column[at_row : at_row + NB], "prow", block % nprow)
    stored = factor_rows(column, corner, block)
    stored = spread(stored, "pcol", block % npcol)
    global_block = jnp.arange(rows) // NB * nprow + myrow
    finished = jnp.where((global_block > block)[:, None], stored, 0.0)
    factor_blocks = finished.reshape(cols // NB, npcol // nprow, NB, NB)
    chosen = lax.dynamic_index_in_dim(factor_blocks, mycol // nprow, 1, keepdims=False)
    across = spread(chosen.reshape(cols, NB), "prow", mycol % nprow)
    return (stored, finished, across)


def subtract(matrix, finished, across, first, last):
    product = lax.dot_general(
        finished,
        across,
        (((1,), (1,)), ((), ())),
        precision=HIGHEST_PRECISION,
        preferred_element_type=jnp.float32,
    )
    return matrix.at[:, first:last].set(matrix - product)


def place_column(matrix, stored, block):
    npcol = lax.axis_size("pcol")
    mycol = lax.axis_index("pcol")
    at_column = block // npcol * NB
    current = matrix[:, at_column : at_column + NB]
    return matrix.at[:, at_column : at_column + NB].set(
        jnp.where(mycol == block % npcol, stored, current)
    )


def shards(matrix):
    cols = matrix.shape[1]
    for block in range(STEPS):
        stored, finished, across = factor_panel(matrix, block)
        matrix = subtract(matrix, finished, across, 0, cols)
        matrix = place_column(matrix, stored, block)
    return matrix


def solution(mesh):
    return jax.shard_map(
        shards,
        mesh=mesh,
        in_specs=(P("prow", "pcol"),),
        out_specs=P("prow", "pcol"),
        check_vma=False,
    )
```

profile of v0, /device:TPU:22, one launch (start us, length us, event | category | flops | bytes accessed | tf_op | source)
XLA Modules:
  0.0 1263.9 jit_solution(9377193175351166299)
XLA Ops:
  19.2 58.0 %all-reduce.14.cloned.1.call-done = f32[256,256]{0,1:T(8,128)} async-done(((f32[256,256]{0,1:T(8,128)}), f32[256,256]{0,1:T(8,128)}) %all-reduce.14.cloned.1.call-update) | async-done | bytes 262160 | tf_op jit(solution)/shard_map/psum | solution.py:15
  101.3 11.7 cholesky.231
  120.1 19.7 %custom-call.18 = f32[2,128,128]{1,2,0:T(8,128)S(1)} custom-call(f32[2,128,128]{2,1,0:T(8,128)S(1)} %get-tuple-element.161), custom_call_target="InvertDiagBlocksLowerTriangular" | custom-call | tf_op jit(solution)/shard_map/jit(_solve_triangular)/triangular_solve | solution.py:22
  146.8 90.6 %all-reduce.16.cloned.1.call-done = f32[2048,256]{0,1:T(8,128)} async-done(((f32[2048,256]{0,1:T(8,128)}), f32[2048,256]{0,1:T(8,128)}) %all-reduce.16.cloned.1.call-update) | async-done | bytes 2097168 | tf_op jit(solution)/shard_map/psum | solution.py:15
  249.2 60.0 %all-reduce.18.cloned.1.call-done = f32[1024,256]{0,1:T(8,128)} async-done(((f32[1024,256]{0,1:T(8,128)}), f32[1024,256]{0,1:T(8,128)}) %all-reduce.18.cloned.1.call-update) | async-done | bytes 1048592 | tf_op jit(solution)/shard_map/psum | solution.py:15
  309.2 11.8 convolution_subtract_fusion.3
  326.0 59.0 %all-reduce.20.cloned.1.call-done = f32[256,256]{0,1:T(8,128)} async-done(((f32[256,256]{0,1:T(8,128)}), f32[256,256]{0,1:T(8,128)}) %all-reduce.20.cloned.1.call-update) | async-done | bytes 262160 | tf_op jit(solution)/shard_map/psum | solution.py:15
  409.2 11.7 cholesky.265
  428.7 19.7 %custom-call.20 = f32[2,128,128]{1,2,0:T(8,128)S(1)} custom-call(f32[2,128,128]{2,1,0:T(8,128)S(1)} %get-tuple-element.162), custom_call_target="InvertDiagBlocksLowerTriangular" | custom-call | tf_op jit(solution)/shard_map/jit(_solve_triangular)/triangular_solve | solution.py:22
  454.5 90.6 %all-reduce.22.cloned.1.call-done = f32[2048,256]{0,1:T(8,128)} async-done(((f32[2048,256]{0,1:T(8,128)}), f32[2048,256]{0,1:T(8,128)}) %all-reduce.22.cloned.1.call-update) | async-done | bytes 2097168 | tf_op jit(solution)/shard_map/psum | solution.py:15
  555.9 60.7 %all-reduce.24.cloned.1.call-done = f32[1024,256]{0,1:T(8,128)} async-done(((f32[1024,256]{0,1:T(8,128)}), f32[1024,256]{0,1:T(8,128)}) %all-reduce.24.cloned.1.call-update) | async-done | bytes 1048592 | tf_op jit(solution)/shard_map/psum | solution.py:15
  616.6 11.9 convolution_subtract_fusion.2
  633.3 59.2 %all-reduce.26.cloned.1.call-done = f32[256,256]{0,1:T(8,128)} async-done(((f32[256,256]{0,1:T(8,128)}), f32[256,256]{0,1:T(8,128)}) %all-reduce.26.cloned.1.call-update) | async-done | bytes 262160 | tf_op jit(solution)/shard_map/psum | solution.py:15
  716.7 11.7 cholesky.299
  736.2 19.7 %custom-call.22 = f32[2,128,128]{1,2,0:T(8,128)S(1)} custom-call(f32[2,128,128]{2,1,0:T(8,128)S(1)} %get-tuple-element.163), custom_call_target="InvertDiagBlocksLowerTriangular" | custom-call | tf_op jit(solution)/shard_map/jit(_solve_triangular)/triangular_solve | solution.py:22
  762.0 90.6 %all-reduce.28.cloned.1.call-done = f32[2048,256]{0,1:T(8,128)} async-done(((f32[2048,256]{0,1:T(8,128)}), f32[2048,256]{0,1:T(8,128)}) %all-reduce.28.cloned.1.call-update) | async-done | bytes 2097168 | tf_op jit(solution)/shard_map/psum | solution.py:15
  863.4 60.7 %all-reduce.30.cloned.1.call-done = f32[1024,256]{0,1:T(8,128)} async-done(((f32[1024,256]{0,1:T(8,128)}), f32[1024,256]{0,1:T(8,128)}) %all-reduce.30.cloned.1.call-update) | async-done | bytes 1048592 | tf_op jit(solution)/shard_map/psum | solution.py:15
  924.1 11.9 convolution_subtract_fusion.1
  940.8 59.2 %all-reduce.32.cloned.1.call-done = f32[256,256]{0,1:T(8,128)} async-done(((f32[256,256]{0,1:T(8,128)}), f32[256,256]{0,1:T(8,128)}) %all-reduce.32.cloned.1.call-update) | async-done | bytes 262160 | tf_op jit(solution)/shard_map/psum | solution.py:15
  1024.2 11.7 cholesky.333
  1043.5 19.7 %custom-call.24 = f32[2,128,128]{1,2,0:T(8,128)S(1)} custom-call(f32[2,128,128]{2,1,0:T(8,128)S(1)} %get-tuple-element.164), custom_call_target="InvertDiagBlocksLowerTriangular" | custom-call | tf_op jit(solution)/shard_map/jit(_solve_triangular)/triangular_solve | solution.py:22
  1069.4 90.5 %all-reduce.34.cloned.1.call-done = f32[2048,256]{0,1:T(8,128)} async-done(((f32[2048,256]{0,1:T(8,128)}), f32[2048,256]{0,1:T(8,128)}) %all-reduce.34.cloned.1.call-update) | async-done | bytes 2097168 | tf_op jit(solution)/shard_map/psum | solution.py:15
  1170.9 60.8 %all-reduce.36.cloned.1.call-done = f32[1024,256]{0,1:T(8,128)} async-done(((f32[1024,256]{0,1:T(8,128)}), f32[1024,256]{0,1:T(8,128)}) %all-reduce.36.cloned.1.call-update) | async-done | bytes 1048592 | tf_op jit(solution)/shard_map/psum | solution.py:15
  1231.7 11.7 convolution_subtract_fusion
  (188 shorter events, 247.3 us)
Async XLA Ops:
  6.5 70.6 %all-reduce.14.cloned.1.call-start = ((), (), s32[]{:S(2)}) async-start(), calls=%async_computation | async-start | bytes 524288 | tf_op jit(solution)/shard_map/psum | solution.py:15
  17.4 220.0 %all-reduce.16.cloned.1.call-start = ((), (), s32[]{:S(2)}) async-start(), calls=%async_computation.1 | async-start | bytes 4194304 | tf_op jit(solution)/shard_map/psum | solution.py:15
  142.7 1.1 copy-start.5
  146.7 162.5 %all-reduce.18.cloned.1.call-start = ((), (), s32[]{:S(2)}) async-start(), calls=%async_computation.2 | async-start | bytes 2097152 | tf_op jit(solution)/shard_map/psum | solution.py:15
  248.5 136.6 %all-reduce.20.cloned.1.call-start = ((), (), s32[]{:S(2)}) async-start(), calls=%async_computation.3 | async-start | bytes 524288 | tf_op jit(solution)/shard_map/psum | solution.py:15
  309.2 11.8 copy-start
  325.7 219.4 %all-reduce.22.cloned.1.call-start = ((), (), s32[]{:S(2)}) async-start(), calls=%async_computation.4 | async-start | bytes 4194304 | tf_op jit(solution)/shard_map/psum | solution.py:15
  450.5 1.1 copy-start.6
  454.5 162.1 %all-reduce.24.cloned.1.call-start = ((), (), s32[]{:S(2)}) async-start(), calls=%async_computation.5 | async-start | bytes 2097152 | tf_op jit(solution)/shard_map/psum | solution.py:15
  555.8 136.7 %all-reduce.26.cloned.1.call-start = ((), (), s32[]{:S(2)}) async-start(), calls=%async_computation.6 | async-start | bytes 524288 | tf_op jit(solution)/shard_map/psum | solution.py:15
  616.6 11.9 copy-start.1
  633.2 219.4 %all-reduce.28.cloned.1.call-start = ((), (), s32[]{:S(2)}) async-start(), calls=%async_computation.7 | async-start | bytes 4194304 | tf_op jit(solution)/shard_map/psum | solution.py:15
  758.0 1.1 copy-start.7
  762.0 162.1 %all-reduce.30.cloned.1.call-start = ((), (), s32[]{:S(2)}) async-start(), calls=%async_computation.8 | async-start | bytes 2097152 | tf_op jit(solution)/shard_map/psum | solution.py:15
  863.3 136.7 %all-reduce.32.cloned.1.call-start = ((), (), s32[]{:S(2)}) async-start(), calls=%async_computation.9 | async-start | bytes 524288 | tf_op jit(solution)/shard_map/psum | solution.py:15
  924.1 11.9 copy-start.2
  940.7 219.2 %all-reduce.34.cloned.1.call-start = ((), (), s32[]{:S(2)}) async-start(), calls=%async_computation.10 | async-start | bytes 4194304 | tf_op jit(solution)/shard_map/psum | solution.py:15
  1065.3 1.1 copy-start.4
  1069.3 162.4 %all-reduce.36.cloned.1.call-start = ((), (), s32[]{:S(2)}) async-start(), calls=%async_computation.11 | async-start | bytes 2097152 | tf_op jit(solution)/shard_map/psum | solution.py:15
  1231.7 11.7 copy-start.3
Sparse Core Ops, SparseCore 0:
  17.5 59.6 all-reduce.13
  146.8 90.4 all-reduce.15
  248.6 60.6 all-reduce.17
  325.9 59.1 all-reduce.19
  454.6 90.4 all-reduce.21
  555.9 60.6 all-reduce.23
  633.3 59.1 all-reduce.25
  762.1 90.4 all-reduce.27
  863.4 60.6 all-reduce.29
  940.8 59.1 all-reduce.31
  1069.4 90.4 all-reduce.33
  1171.0 60.6 all-reduce.35
where the time goes:
time: 1280 us; the launch traced here: 1260 us
  waiting for transfers between devices  840 us (66%)
  other arithmetic  278 us (22%)
  matrix products  62.6 us (5%)
  local copies, waits for them, and re-layouts  61.8 us (5%)
  between operations  19.7 us (2%)
    psum x12, waiting for transfers between devices, spread(): return lax.psum(block, axis)  840 us
    another operation x27, other arithmetic, factor_rows(): triangle = jnp.linalg.cholesky(corner)  138 us
    another operation x9, other arithmetic, factor_rows(): solved = jax.scipy.linalg.solve_triangular(triangle, column.T, lower=True).T  81.6 us
    dot_general x4, matrix products, subtract(): lax.dot_general(finished, across, (((1,), (1,)), ((), ())), precision=HIG...  47.4 us
    select_n x12, other arithmetic, spread(): jnp.where(lax.axis_index(axis) == owner, block, jnp.zeros_like(block))  30.5 us
  transfers between devices with their start and end apart: 12, of which 12 were waited for; matrix products, arithmetic and copies ran while one was open for 0% of the time, Pallas kernels for 0%

commit v1 on v0

v1 whole, which is shorter than its diff:
```python
import functools

import jax
import jax.numpy as jnp
from jax import lax
from jax.experimental import pallas as pl
from jax.experimental.pallas import tpu as pltpu
from jax.sharding import PartitionSpec as P

F32 = jnp.float32
BF16 = jnp.bfloat16
MESH = pl.DeviceIdType.MESH

TURNS = ((1, 0), (0, -1), (-1, 0), (0, 1))
PARENT = {
    (0, 1): 0, (1, 0): 2, (0, 3): 0, (3, 0): 2, (1, 1): 2, (1, 3): 2, (3, 3): 1, (3, 1): 3,
    (1, 2): 2, (2, 3): 1, (3, 2): 3, (2, 1): 2, (2, 2): 1, (2, 0): 2, (0, 2): 0,
}


def tree_tables():
    masks, depths = {}, {(0, 0): 0}
    for node in [(0, 0), *PARENT]:
        masks[node] = 0

    def depth(node):
        if node not in depths:
            dy, dz = TURNS[PARENT[node]]
            depths[node] = depth(((node[0] - dy) % 4, (node[1] - dz) % 4)) + 1
        return depths[node]

    for node, turn in PARENT.items():
        dy, dz = TURNS[turn]
        masks[(node[0] - dy) % 4, (node[1] - dz) % 4] |= 1 << turn
        depth(node)
    order = [(a, b) for a in range(4) for b in range(4)]
    return [masks[n] for n in order], [depths[n] for n in order]


MASKS, DEPTHS = tree_tables()
DEEPEST = max(DEPTHS)
LAG = 2
UNIT = 64
SLOTS = (((0, 0), (0, 1), (0, 2), (0, 3), (2, 2), (2, 3)), ((1, 1), (1, 2), (1, 3), (3, 3)))


def place():
    row, col = lax.axis_index("prow"), lax.axis_index("pcol")
    return row // 2, row % 2, col // 4, col % 4


def pick(index, values):
    out = jnp.int32(values[0])
    for i in range(1, len(values)):
        out = jnp.where(index == i, jnp.int32(values[i]), out)
    return out


def roles(y, z):
    table = []
    for s in range(4):
        a, b = y, (z - s + 4) % 4
        line = []
        for t in range(4):
            index = a * 4 + b
            mask, depth = pick(index, MASKS), pick(index, DEPTHS)
            flags = [None] * 4
            for d in range(4):
                flags[(d + t) % 4] = (mask // (1 << d)) % 2
            line.append((depth, flags))
            a, b = (4 - b) % 4, a
        table.append(line)
    return table


def comm_kernel(k_ref, ar_ref, z_ref, xs, xr, cs, cr, ks, kr, ps, pr, rs, rr, ls):
    x, core, y, z = place()
    mycol = y * 4 + z
    table = roles(y, z)

    def at(px, pcore, py, pz):
        return (px * 2 + pcore, py * 4 + pz)

    peer = at(x, 1 - core, y, z)
    others = [at((x + d) % 4, core, y, z) for d in (1, 2, 3)]
    around = [at(x, core, (y + dy + 4) % 4, (z + dz + 4) % 4) for dy, dz in TURNS]
    barrier = pltpu.get_barrier_semaphore()
    for device in [peer, *others, *around]:
        pl.semaphore_signal(barrier, inc=1, device_id=device, device_id_type=MESH)
    pl.semaphore_wait(barrier, 8)

    def remote(src, dst, ssem, rsem, device):
        return pltpu.make_async_remote_copy(src, dst, ssem, rsem, device_id=device, device_id_type=MESH)

    parts = ((0, 256), (256, 768))

    def top_rows(owner, part):
        first, width = parts[part]
        return z_ref.at[pl.ds(pl.multiple_of(owner * 256, 256), 256), pl.ds(1024 + first, width)]

    def own_top(part):
        first, width = parts[part]
        return k_ref.at[pl.ds(0, 256), pl.ds(first, width)]

    def x_copy(o, part, i):
        return remote(own_top(part), top_rows(o * 2 + core, part), xs.at[part, i], xr.at[o, part], others[i])

    def x_keep(o, part):
        return pltpu.make_async_copy(own_top(part), top_rows(o * 2 + core, part), ls.at[part])

    def peer_first(o, part):
        return remote(own_top(part), top_rows(o * 2 + core, part), cs.at[o, part], cr.at[o, part], peer)

    def peer_next(o, part, owner_core):
        block = top_rows(o * 2 + owner_core, part)
        return remote(block, block, cs.at[o, part], cr.at[o, part], peer)

    for part in range(2):
        for o in range(2):

            @pl.when(x == o)
            def _():
                for i in range(3):
                    x_copy(o, part, i).start()
                peer_first(o, part).start()
                x_keep(o, part).start()

    keep_column = pltpu.make_async_copy(
        k_ref.at[:, pl.ds(0, 256)], ar_ref.at[:, pl.ds(pl.multiple_of(z * 256, 256), 256)], ls.at[2]
    )

    @pl.when(y == 0)
    def _():
        keep_column.start()

    def x_arrive(part):
        for o in range(2):

            @pl.when(x != o)
            def _():
                x_copy(o, part, 0).wait_recv()
                peer_next(o, part, core).start()

            @pl.when(x == o)
            def _():
                x_keep(o, part).wait()

    def peer_arrive(part):
        for o in range(2):
            peer_next(o, part, 1 - core).wait_recv()

    x_arrive(0)

    def slot(i, own):
        first, second = SLOTS if own else SLOTS[::-1]
        if i < len(SLOTS[1]):
            pair = lambda u: jnp.where(core == 0, first[i][u], second[i][u])
            return pair(0), pair(1), None
        full = max(SLOTS, key=len)[i]
        return jnp.int32(full[0]), jnp.int32(full[1]), (core == 0) if own else (core == 1)

    def lead(b, s, t, width=UNIT):
        return z_ref.at[pl.ds(pl.multiple_of(b * 256 + t * UNIT, UNIT), width), pl.ds(pl.multiple_of(s * 256, 256), 256)]

    def lead_own(b, t):
        return z_ref.at[pl.ds(pl.multiple_of(b * 256 + t * UNIT, UNIT), UNIT), pl.ds(1024, 256)]

    def role(s, t):
        depth = table[3][t][0]
        flags = list(table[3][t][1])
        for o in range(3):
            depth = jnp.where(s == o, table[o][t][0], depth)
            flags = [jnp.where(s == o, a, b) for a, b in zip(table[o][t][1], flags)]
        return depth, flags

    lead_roles = []
    for i in range(6):
        b, s, used = slot(i, True)
        lead_roles.append([role(s, t) for t in range(4)])

    def lead_tick(tick):
        for i in range(6):
            b, s, used = slot(i, True)
            for t in range(4):
                depth, flags = lead_roles[i][t]
                now = tick == i + LAG * depth
                if used is not None:
                    now = now & used
                block = lead(b, s, t)

                @pl.when(now & (depth == 0))
                def _():
                    for d in range(4):

                        @pl.when(flags[d] == 1)
                        def _():
                            remote(lead_own(b, t), block, ks.at[i, t, d], kr.at[i, t], around[d]).start()

                @pl.when(now & (depth != 0))
                def _():
                    remote(block, block, ks.at[i, t, 0], kr.at[i, t], peer).wait_recv()
                    for d in range(4):

                        @pl.when(flags[d] == 1)
                        def _():
                            remote(block, block, ks.at[i, t, d], kr.at[i, t], around[d]).start()

                    remote(block, block, ps.at[i, t], pr.at[i, t], peer).start()

    def lead_finish_sends():
        for i in range(6):
            b, s, used = slot(i, True)
            for t in range(4):
                depth, flags = lead_roles[i][t]
                block = lead(b, s, t)
                ok = jnp.bool_(True) if used is None else used
                for d in range(4):

                    @pl.when(ok & (flags[d] == 1))
                    def _():
                        remote(block, block, ks.at[i, t, d], kr.at[i, t], around[d]).wait_send()

                @pl.when(ok & (depth != 0))
                def _():
                    remote(block, block, ps.at[i, t], pr.at[i, t], peer).wait_send()

    def lead_arrive():
        for i in range(6):
            b, s, used = slot(i, False)
            ok = mycol != s
            if used is not None:
                ok = ok & used
            for t in range(4):
                block = lead(b, s, t)

                @pl.when(ok)
                def _():
                    remote(block, block, ps.at[i, t], pr.at[i, t], peer).wait_recv()

    def unit(s, t, q):
        return pl.ds(pl.multiple_of(t * 512 + q * UNIT, UNIT), UNIT), pl.ds(s * 256, 256)

    def row_tick(tick):
        for s in range(4):
            for t in range(4):
                depth, flags = table[s][t]
                q = tick - (6 + 8 * s) - LAG * depth
                now = (q >= 0) & (q < 8)
                rows, cols = unit(s, t, q)

                @pl.when(now & (depth == 0))
                def _():
                    for d in range(4):

                        @pl.when(flags[d] == 1)
                        def _():
                            remote(
                                k_ref.at[rows, pl.ds(0, 256)], ar_ref.at[rows, cols], rs.at[s, t, d], rr.at[s, t, q], around[d]
                            ).start()

                @pl.when(now & (depth != 0))
                def _():
                    block = ar_ref.at[rows, cols]
                    remote(block, block, rs.at[s, t, 0], rr.at[s, t, q], peer).wait_recv()
                    for d in range(4):

                        @pl.when(flags[d] == 1)
                        def _():
                            remote(block, block, rs.at[s, t, d], rr.at[s, t, q], around[d]).start()

    def row_finish_sends():
        for s in range(4):
            for t in range(4):
                depth, flags = table[s][t]
                block = ar_ref.at[pl.ds(t * 512, 512), pl.ds(s * 256, 256)]
                for d in range(4):

                    @pl.when(flags[d] == 1)
                    def _():
                        remote(block, block, rs.at[s, t, d], rr.at[s, t, 0], around[d]).wait_send()

    lead_ticks = 6 + LAG * DEEPEST
    row_ticks = 6 + 32 + LAG * DEEPEST

    @pl.loop(0, lead_ticks)
    def _(tick):
        lead_tick(tick)
        row_tick(tick)

    peer_arrive(0)

    @pl.when(y == 0)
    def _():
        pltpu.make_async_copy(z_ref.at[:, pl.ds(1024, 256)], z_ref.at[:, pl.ds(pl.multiple_of(z * 256, 256), 256)], ls.at[0]).start()

    x_arrive(1)
    lead_arrive()

    @pl.loop(lead_ticks, row_ticks)
    def _(tick):
        row_tick(tick)

    @pl.when(y == 0)
    def _():
        keep_column.wait()
        pltpu.make_async_copy(z_ref.at[:, pl.ds(1024, 256)], z_ref.at[:, pl.ds(pl.multiple_of(z * 256, 256), 256)], ls.at[0]).wait()

    peer_arrive(1)
    for part in range(2):
        for o in range(2):

            @pl.when(x == o)
            def _():
                for i in range(3):
                    x_copy(o, part, i).wait_send()
                peer_first(o, part).wait_send()

            @pl.when(x != o)
            def _():
                peer_next(o, part, core).wait_send()

    lead_finish_sends()
    row_finish_sends()


def gather(matrix):
    sems = [(2, 3), (2, 2), (2, 2), (2, 2), (6, 4, 4), (6, 4), (6, 4), (6, 4), (4, 4, 4), (4, 4, 8), (3,)]
    return pl.pallas_call(
        comm_kernel,
        out_shape=[jax.ShapeDtypeStruct((2048, 1024), F32), jax.ShapeDtypeStruct((1024, 2048), F32)],
        in_specs=[pl.BlockSpec(memory_space=pl.ANY)],
        out_specs=[pl.BlockSpec(memory_space=pl.ANY)] * 2,
        scratch_shapes=[pltpu.SemaphoreType.DMA(s) for s in sems],
        compiler_params=pltpu.CompilerParams(collective_id=0, has_side_effects=True),
        name="gather",
    )(matrix)


def split(a):
    high = a.astype(BF16)
    return high, (a - high.astype(F32)).astype(BF16)


def product(a, b):
    dot = functools.partial(jnp.dot, preferred_element_type=F32)
    return dot(a[0], b[0]) + (dot(a[0], b[1]) + dot(a[1], b[0]))


def lanes(block, j):
    return jnp.take_along_axis(block, jnp.full((8, 128), j, jnp.int32), axis=1)


def rows_of(block, i):
    return jnp.broadcast_to(block[i : i + 1], (8, 128))


def triangle128(load, upper_ref, inverse_ref):
    lane = lax.broadcasted_iota(jnp.int32, (8, 128), 1)
    sub = lax.broadcasted_iota(jnp.int32, (8, 128), 0)
    strips = [load(v) for v in range(16)]
    for b in range(16):
        first, count = 8 * b, 16 - b
        inside = (lane >= first) & (lane < first + 8)
        columns = [lanes(strips[b], first + i) for i in range(8)]
        pivot = [[rows_of(columns[i], k) for k in range(8)] for i in range(8)]
        start = jnp.where(inside, jnp.where(lane == sub + first, 1.0, 0.0), strips[b])
        rows = [rows_of(start, i) for i in range(8)]
        if count > 1:
            below = [lanes(strips[b + 1], first + i) for i in range(8)]
            after = jnp.where(inside, 0.0, strips[b + 1])
        scales, factors = [], []
        for i in range(8):
            scale = 1.0 / pivot[i][i]
            scales.append(scale)
            factor = [None] * 8
            for j in range(i + 1, 8):
                factor[j] = pivot[i][j] * scale
            factors.append(factor)
            for j in range(i + 1, 8):
                pivot[j][j] = pivot[j][j] - (pivot[i][j] * pivot[i][j]) * scale
                for k in range(j + 1, 8):
                    pivot[j][k] = pivot[j][k] - factor[j] * pivot[i][k]
                rows[j] = rows[j] - factor[j] * rows[i]
            if count > 1:
                weight = below[i] * scale
                for k in range(i + 1, 8):
                    below[k] = below[k] - weight * pivot[i][k]
                after = after - weight * rows[i]
        if count > 2:
            solved = [None] * 8
            for i in range(7, -1, -1):
                row = rows[i] * scales[i]
                for k in range(i + 1, 8):
                    row = row - factors[i][k] * solved[k]
                solved[i] = row
            for v in range(2, count):
                strip = jnp.where(inside, 0.0, strips[b + v])
                for i in range(8):
                    strip = strip - lanes(strips[b + v], first + i) * solved[i]
                strips[b + v] = strip
        if count > 1:
            strips[b + 1] = after
        inverse = upper = None
        for i in range(7, -1, -1):
            root = lax.rsqrt(pivot[i][i])
            left = rows[i] * root
            right = left
            for k in range(i, 8):
                right = jnp.where(lane == first + k, pivot[i][k] * root, right)
            inverse = left if inverse is None else jnp.where(sub == i, left, inverse)
            upper = right if upper is None else jnp.where(sub == i, right, upper)
        upper_ref[first : first + 8, :] = jnp.where(lane >= sub + first, upper, 0.0)
        inverse_ref[first : first + 8, :] = jnp.where(lane <= sub + first, inverse, 0.0)


TILE = 512


def factor_kernel(z_ref, wh_ref, wl_ref, top_ref, z, inverse, upper, ph, pw):
    row, col = lax.axis_index("prow"), lax.axis_index("pcol")
    z[...] = z_ref[...]

    @pl.loop(0, 4)
    def _(step):
        o = pl.multiple_of(step * 256, 256)

        @pl.when(row == step)
        def _():
            top_ref[...] = z[pl.ds(o, 256), 1024:2048]

        for half in range(2):
            at = pl.multiple_of(o + 128 * half, 128)
            diagonal = (pl.ds(at, 128), pl.ds(at, 128))
            triangle128(
                lambda v: z[pl.ds(pl.multiple_of(at + 8 * v, 8), 8), pl.ds(at, 128)],
                upper,
                inverse.at[step * 2 + half],
            )
            scale = split(inverse[step * 2 + half])

            @pl.loop(0, 2048, step=TILE)
            def _(c):
                cols = pl.ds(pl.multiple_of(c, TILE), TILE)
                z[pl.ds(at, 128), cols] = product(scale, split(z[pl.ds(at, 128), cols]))

            z[diagonal] = upper[...]
            if half == 0:
                next_at = pl.multiple_of(o + 128, 128)
                side = split(z[pl.ds(at, 128), pl.ds(next_at, 128)].T)

                @pl.loop(0, 2048, step=TILE)
                def _(c):
                    cols = pl.ds(pl.multiple_of(c, TILE), TILE)
                    z[pl.ds(next_at, 128), cols] -= product(side, split(z[pl.ds(at, 128), cols]))

            else:
                z[pl.ds(at, 128), pl.ds(o, 128)] = jnp.zeros((128, 128), F32)

        @pl.loop(0, 2048, step=TILE)
        def _(c):
            cols = pl.ds(pl.multiple_of(c, TILE), TILE)
            ph[:, cols], pw[:, cols] = split(z[pl.ds(o, 256), cols])

        @pl.loop(step + 1, 4)
        def _(i):
            at = pl.multiple_of(i * 256, 256)
            side = split(z[pl.ds(o, 256), pl.ds(at, 256)].T)

            @pl.loop(0, 2048, step=TILE)
            def _(c):
                cols = pl.ds(pl.multiple_of(c, TILE), TILE)
                z[pl.ds(at, 256), cols] -= product(side, (ph[:, cols], pw[:, cols]))

    @pl.when((col < 4) & (row < 4) & (row >= col))
    def _():
        block = z[pl.ds(pl.multiple_of(jnp.minimum(col, 3) * 256, 256), 256), pl.ds(pl.multiple_of(jnp.minimum(row, 3) * 256, 256), 256)]
        top_ref[:, 0:256] = block.T

    @pl.when((col < 4) & (row < col))
    def _():
        top_ref[:, 0:256] = jnp.zeros((256, 256), F32)

    @pl.when(col < 4)
    def _():
        a = lax.broadcasted_iota(jnp.int32, (1024, 256), 0)
        b = lax.broadcasted_iota(jnp.int32, (1024, 256), 1)
        z[:, 1024:1280] = jnp.where(a == b + col * 256, -1.0, 0.0)

    for step in range(3, -1, -1):
        o = 256 * step
        side = split(z[o : o + 256, o + 256 : 1024]) if step < 3 else None
        first = split(inverse[2 * step].T)
        second = split(inverse[2 * step + 1].T)
        between = split(z[o : o + 128, o + 128 : o + 256])

        @pl.loop(0, 1024, step=TILE)
        def _(c):
            cols = pl.ds(pl.multiple_of(c, TILE), TILE)
            mine = z[o : o + 256, pl.ds(pl.multiple_of(c + 1024, TILE), TILE)]
            if step < 3:
                mine = mine - product(side, (wh_ref[o + 256 : 1024, cols], wl_ref[o + 256 : 1024, cols]))
            low = split(product(second, split(mine[128:])))
            wh_ref[o + 128 : o + 256, cols], wl_ref[o + 128 : o + 256, cols] = low
            high = split(product(first, split(mine[:128] - product(between, low))))
            wh_ref[o : o + 128, cols], wl_ref[o : o + 128, cols] = high


def weights(z):
    return pl.pallas_call(
        factor_kernel,
        out_shape=[
            jax.ShapeDtypeStruct((1024, 1024), BF16),
            jax.ShapeDtypeStruct((1024, 1024), BF16),
            jax.ShapeDtypeStruct((256, 1024), F32),
        ],
        scratch_shapes=[
            pltpu.VMEM((1024, 2048), F32),
            pltpu.VMEM((8, 128, 128), F32),
            pltpu.VMEM((128, 128), F32),
            pltpu.VMEM((256, 2048), BF16),
            pltpu.VMEM((256, 2048), BF16),
        ],
        compiler_params=pltpu.CompilerParams(vmem_limit_bytes=52 << 20),
        name="weights",
    )(z)


def update_kernel(m_ref, a_ref, wh_ref, wl_ref, top_ref, out_ref):
    row, col = lax.axis_index("prow"), lax.axis_index("pcol")
    out_ref[...] = m_ref[...]

    @pl.when(col < 4)
    def _():
        out_ref[:, 0:256] = jnp.zeros((256, 256), F32)

    out_ref[...] -= product(split(a_ref[...]), (wh_ref[...], wl_ref[...]))

    @pl.when((pl.program_id(0) == 0) & (row < 4))
    def _():
        out_ref[...] = top_ref[...]


def update(matrix, column, wh, wl, top):
    tile = pl.BlockSpec((256, 1024), lambda i: (i, 0))
    whole = lambda shape: pl.BlockSpec(shape, lambda i: (0, 0))
    return pl.pallas_call(
        update_kernel,
        grid=(8,),
        out_shape=jax.ShapeDtypeStruct((2048, 1024), F32),
        in_specs=[tile, tile, whole((1024, 1024)), whole((1024, 1024)), whole((256, 1024))],
        out_specs=tile,
        compiler_params=pltpu.CompilerParams(vmem_limit_bytes=48 << 20),
        name="update",
    )(matrix, column, wh, wl, top)


def shards(matrix):
    column, z = gather(matrix)
    wh, wl, top = weights(z)
    return update(matrix, column, wh, wl, top)


def solution(mesh):
    return jax.shard_map(
        shards,
        mesh=mesh,
        in_specs=(P("prow", "pcol"),),
        out_specs=P("prow", "pcol"),
        check_vma=False,
    )
```

time: 1280 us -> 222 us (0.17)
  the two profiles are of different devices: /device:TPU:22 before, /device:TPU:1 now
where the time goes in v1:
time: 222 us
  Pallas kernels  218 us (98%)
  local copies, waits for them, and re-layouts  3.18 us (1%)
    pallas_call x1, Pallas kernels, gather(): pl.pallas_call(comm_kernel, out_shape=[jax.ShapeDtypeStruct((2048, 1024),...  137 us
    pallas_call x1, Pallas kernels, weights(): pl.pallas_call(factor_kernel, out_shape=[jax.ShapeDtypeStruct((1024, 1024...  63.7 us
    pallas_call x1, Pallas kernels, update(): pl.pallas_call(update_kernel, grid=(8,), out_shape=jax.ShapeDtypeStruct((...  17.8 us

profile of v1, /device:TPU:1, one launch (start us, length us, event | category | flops | bytes accessed | tf_op | source)
XLA Modules:
  0.0 221.7 jit_solution(13005624055507810742)
XLA Ops:
  0.0 137.0 %gather.1 = (f32[2048,1024]{1,0:T(8,128)}, f32[1024,2048]{1,0:T(8,128)}) custom-call(f32[2048,1024]{1,0:T(8,128)} %m_ref.1), custom_call_target="tpu_custom_call" | custom-call | tf_op jit(solution)/shard_map/gather/pallas_call | solution.py:328
  137.0 63.7 %weights.1 = (bf16[1024,1024]{1,0:T(8,128)(2,1)}, bf16[1024,1024]{1,0:T(8,128)(2,1)}, f32[256,1024]{1,0:T(8,128)S(1)}) custom-call(f32[1024,2048]{1,0:T(8,128)} %get-tuple-element.11.z_ref), custom_call_target="tpu_custom_call" | custom-call | tf_op jit(solution)/shard_map/weights/pallas_call | solution.py:509
  200.7 0.0 copy-start
  200.7 1.6 copy-done
  202.3 0.0 copy-start.1
  202.3 1.6 copy-done.1
  203.9 17.8 %update.1 = f32[2048,1024]{1,0:T(8,128)} custom-call(f32[2048,1024]{1,0:T(8,128)} %m_ref.1, f32[2048,1024]{1,0:T(8,128)} %get-tuple-element.10.a_ref, bf16[1024,1024]{1,0:T(8,128)(2,1)S(1)} %copy-done, bf16[1024,1024]{1,0:T(8,128)(2,1)S(1)} %copy-done.1, f32[256,1024]{1,0:T(8,128)S(1)} %get-tuple-element.14.top_ref), custom_call_target="tpu_custom_call" | custom-call | tf_op jit(solution)/shard_map/update/pallas_call | solution.py:546
Async XLA Ops:
  200.7 1.6 copy-start
  202.3 1.6 copy-start.1

commit v2 on v0

v2 whole, which is shorter than its diff:
```python
import functools

import jax
import jax.numpy as jnp
from jax import lax
from jax.experimental import pallas as pl
from jax.experimental.pallas import tpu as pltpu
from jax.sharding import PartitionSpec as P

F32 = jnp.float32
BF16 = jnp.bfloat16
MESH = pl.DeviceIdType.MESH

TURNS = ((1, 0), (0, -1), (-1, 0), (0, 1))
PARENT = {
    (0, 1): 0, (1, 0): 2, (0, 3): 0, (3, 0): 2, (1, 1): 2, (1, 3): 2, (3, 3): 1, (3, 1): 3,
    (1, 2): 2, (2, 3): 1, (3, 2): 3, (2, 1): 2, (2, 2): 1, (2, 0): 2, (0, 2): 0,
}


def tree_children():
    trees = []
    parent = dict(PARENT)
    for _ in range(4):
        children = {(a, b): [] for a in range(4) for b in range(4)}
        for node, turn in parent.items():
            dy, dz = TURNS[turn]
            children[(node[0] - dy) % 4, (node[1] - dz) % 4].append(turn)
        trees.append(children)
        parent = {(n[1] % 4, -n[0] % 4): (d + 1) % 4 for n, d in parent.items()}
    return trees


CHILDREN = tree_children()
UNIT = 64
LEAD = 2

PREFIX = 48
ORDER = (
    (
        8, 72, 136, 200, 73, 203, 74, 202, 0, 64, 128, 192, 4, 68, 132, 196, 201, 75, 9, 137,
        11, 139, 65, 195, 69, 199, 10, 138, 66, 194, 70, 198, 193, 67, 129, 131, 1, 3, 197, 71,
        5, 133, 7, 135, 130, 2, 6, 134, 12, 76, 140, 204, 16, 80, 144, 208, 20, 84, 148, 212,
        24, 88, 152, 216, 28, 92, 156, 220, 32, 96, 160, 224, 36, 100, 164, 228, 77, 207, 81, 211,
        85, 215, 89, 219, 93, 223, 13, 141, 15, 143, 97, 227, 101, 231, 17, 145, 19, 147, 78, 206,
        82, 210, 149, 23, 21, 151, 86, 214, 14, 90, 218, 142, 153, 27, 94, 222, 25, 98, 226, 155,
        157, 31, 102, 230, 18, 205, 79, 146, 161, 35, 209, 83, 29, 159, 213, 87, 165, 39, 217, 91,
        22, 150, 33, 163, 221, 95, 225, 99, 229, 103, 26, 154, 37, 167, 30, 158, 34, 162, 38, 166,
    ),
    (
        136, 137, 139, 73, 203, 8, 202, 72, 200, 74, 138, 128, 132, 201, 9, 11, 75, 129, 131, 65,
        195, 133, 135, 69, 10, 199, 64, 66, 194, 0, 192, 130, 4, 198, 68, 70, 196, 134, 193, 1,
        3, 67, 197, 71, 5, 7, 2, 6, 140, 144, 148, 141, 143, 152, 145, 147, 156, 149, 12, 151,
        160, 142, 153, 16, 164, 155, 157, 20, 146, 161, 15, 77, 207, 159, 165, 13, 19, 150, 81, 211,
        163, 78, 24, 204, 85, 215, 167, 208, 82, 154, 14, 17, 23, 76, 79, 89, 219, 158, 28, 212,
        86, 80, 93, 223, 83, 162, 18, 21, 27, 84, 32, 97, 227, 216, 90, 166, 88, 231, 22, 101,
        87, 92, 220, 94, 206, 96, 31, 36, 25, 210, 100, 205, 224, 98, 214, 26, 91, 35, 218, 209,
        222, 213, 228, 102, 29, 226, 217, 95, 39, 30, 230, 221, 33, 99, 225, 229, 34, 103, 37, 38,
    ),
    (
        8, 136, 137, 11, 9, 73, 139, 203, 74, 202, 72, 200, 10, 138, 0, 128, 4, 132, 201, 75,
        129, 3, 1, 65, 131, 195, 133, 7, 5, 69, 135, 199, 194, 130, 66, 64, 2, 192, 198, 70,
        68, 196, 6, 134, 67, 193, 71, 197, 12, 140, 16, 144, 15, 141, 20, 148, 13, 143, 19, 145,
        24, 152, 149, 23, 14, 142, 17, 147, 28, 156, 18, 146, 27, 153, 21, 151, 32, 160, 22, 150,
        31, 157, 36, 164, 25, 155, 26, 154, 35, 161, 207, 77, 29, 159, 39, 165, 211, 81, 30, 158,
        33, 163, 76, 204, 34, 162, 215, 85, 37, 167, 219, 89, 80, 38, 208, 166, 223, 93, 84, 212,
        227, 97, 88, 216, 92, 220, 231, 101, 78, 206, 96, 224, 82, 210, 100, 228, 205, 79, 86, 214,
        90, 218, 209, 83, 94, 222, 213, 87, 98, 226, 217, 91, 102, 230, 221, 95, 225, 99, 229, 103,
    ),
    (
        8, 9, 11, 73, 203, 136, 74, 72, 200, 10, 202, 0, 4, 75, 137, 139, 1, 3, 201, 65,
        195, 5, 7, 69, 138, 199, 64, 2, 128, 66, 192, 194, 132, 70, 68, 6, 196, 198, 129, 67,
        193, 131, 71, 133, 197, 135, 130, 134, 12, 16, 20, 13, 15, 24, 17, 19, 28, 23, 140, 21,
        32, 14, 27, 144, 36, 25, 31, 148, 18, 35, 141, 77, 207, 29, 39, 143, 145, 22, 81, 211,
        33, 206, 152, 76, 85, 215, 37, 80, 210, 26, 142, 147, 149, 204, 205, 89, 219, 30, 156, 84,
        214, 208, 93, 223, 209, 34, 146, 151, 153, 212, 160, 97, 227, 88, 218, 38, 216, 101, 150, 231,
        213, 92, 220, 222, 78, 224, 157, 164, 155, 82, 228, 79, 96, 226, 86, 154, 217, 161, 90, 83,
        94, 87, 100, 230, 159, 98, 91, 221, 165, 158, 102, 95, 163, 225, 99, 103, 162, 229, 167, 166,
    ),
)


def place():
    row, col = lax.axis_index("prow"), lax.axis_index("pcol")
    return row // 2, row % 2, col // 4, col % 4


def pick(index, values):
    out = jnp.int32(values[0])
    for i in range(1, len(values)):
        if values[i] != values[0] or len(set(values)) > 1:
            out = jnp.where(index == i, jnp.int32(values[i]), out)
    return out


def packed(y, code):
    dz, tree = code % 4, code // 64
    links = sum(1 << d for d in CHILDREN[tree][y, dz])
    return code + 256 * ((y == 0 and dz == 0) + 2 * links)


def split(a):
    high = a.astype(BF16)
    return high, (a - high.astype(F32)).astype(BF16)


def product(a, b):
    dot = functools.partial(jnp.dot, preferred_element_type=F32)
    return dot(a[0], b[0]) + (dot(a[0], b[1]) + dot(a[1], b[0]))


def lanes(block, j):
    return jnp.take_along_axis(block, jnp.full((8, 128), j, jnp.int32), axis=1)


def rows_of(block, i):
    return jnp.broadcast_to(block[i : i + 1], (8, 128))


def triangle128(load, upper_ref, inverse_ref, hook):
    lane = lax.broadcasted_iota(jnp.int32, (8, 128), 1)
    sub = lax.broadcasted_iota(jnp.int32, (8, 128), 0)
    strips = [load(v) for v in range(16)]
    for b in range(16):
        first, count = 8 * b, 16 - b
        inside = (lane >= first) & (lane < first + 8)
        columns = [lanes(strips[b], first + i) for i in range(8)]
        pivot = [[rows_of(columns[i], k) for k in range(8)] for i in range(8)]
        start = jnp.where(inside, jnp.where(lane == sub + first, 1.0, 0.0), strips[b])
        rows = [rows_of(start, i) for i in range(8)]
        if count > 1:
            below = [lanes(strips[b + 1], first + i) for i in range(8)]
            after = jnp.where(inside, 0.0, strips[b + 1])
        scales, factors = [], []
        for i in range(8):
            scale = 1.0 / pivot[i][i]
            scales.append(scale)
            factor = [None] * 8
            for j in range(i + 1, 8):
                factor[j] = pivot[i][j] * scale
            factors.append(factor)
            for j in range(i + 1, 8):
                pivot[j][j] = pivot[j][j] - (pivot[i][j] * pivot[i][j]) * scale
                for k in range(j + 1, 8):
                    pivot[j][k] = pivot[j][k] - factor[j] * pivot[i][k]
                rows[j] = rows[j] - factor[j] * rows[i]
            if count > 1:
                weight = below[i] * scale
                for k in range(i + 1, 8):
                    below[k] = below[k] - weight * pivot[i][k]
                after = after - weight * rows[i]
        if count > 2:
            solved = [None] * 8
            for i in range(7, -1, -1):
                row = rows[i] * scales[i]
                for k in range(i + 1, 8):
                    row = row - factors[i][k] * solved[k]
                solved[i] = row
            for v in range(2, count):
                strip = jnp.where(inside, 0.0, strips[b + v])
                for i in range(8):
                    strip = strip - lanes(strips[b + v], first + i) * solved[i]
                strips[b + v] = strip
        if count > 1:
            strips[b + 1] = after
        hook(b)
        inverse = upper = None
        for i in range(7, -1, -1):
            root = lax.rsqrt(pivot[i][i])
            left = rows[i] * root
            right = left
            for k in range(i, 8):
                right = jnp.where(lane == first + k, pivot[i][k] * root, right)
            inverse = left if inverse is None else jnp.where(sub == i, left, inverse)
            upper = right if upper is None else jnp.where(sub == i, right, upper)
        upper_ref[first : first + 8, :] = jnp.where(lane >= sub + first, upper, 0.0)
        inverse_ref[first : first + 8, :] = jnp.where(lane <= sub + first, inverse, 0.0)


TILE = 512


def panels_kernel(
    k_ref, ar_out, wh_ref, wl_ref, top_ref, ar, z, inverse, upper, inverse_high, inverse_low, order, xs, xr, cs, cr, ks, kr, ps, pr, rs, rr, ls
):
    x, core, y, zz = place()
    row, col = x * 2 + core, y * 4 + zz

    def at(px, pcore, py, pz):
        return (px * 2 + pcore, py * 4 + pz)

    peer = at(x, 1 - core, y, zz)
    after, before = at((x + 1) % 4, core, y, zz), at((x + 3) % 4, core, y, zz)
    around = [at(x, core, (y + dy + 4) % 4, (zz + dz + 4) % 4) for dy, dz in TURNS]
    barrier = pltpu.get_barrier_semaphore()
    for device in [peer, after, before, *around]:
        pl.semaphore_signal(barrier, inc=1, device_id=device, device_id_type=MESH)

    keep_column = pltpu.make_async_copy(k_ref.at[:, pl.ds(0, 256)], ar.at[zz], ls.at[4])

    @pl.when(y == 0)
    def _():
        keep_column.start()

    for e in range(16 * (LEAD + 8)):
        order[e] = pick(y, [packed(i, ORDER[i][e]) for i in range(4)])

    pl.semaphore_wait(barrier, 7)

    def remote(src, dst, ssem, rsem, device):
        return pltpu.make_async_remote_copy(src, dst, ssem, rsem, device_id=device, device_id_type=MESH)

    def top_rows(o, of_core, part):
        return z.at[pl.ds(pl.multiple_of(o * 512 + of_core * 256, 256), 256), pl.ds(1024 + 256 * part, 256)]

    def own_top(part):
        return k_ref.at[pl.ds(0, 256), pl.ds(256 * part, 256)]

    def x_own(o, part, i):
        return remote(own_top(part), top_rows(o, core, part), xs.at[part, i], xr.at[o, part], (after, before)[i])

    def x_pass(o, part, device):
        block = top_rows(o, core, part)
        return remote(block, block, xs.at[part, 0], xr.at[o, part], device)

    def x_keep(o, part):
        return pltpu.make_async_copy(own_top(part), top_rows(o, core, part), ls.at[part])

    def peer_own(o, part):
        return remote(own_top(part), top_rows(o, core, part), cs.at[o, part], cr.at[o, part], peer)

    def peer_pass(o, part, of_core):
        block = top_rows(o, of_core, part)
        return remote(block, block, cs.at[o, part], cr.at[o, part], peer)

    def x_start(part):
        for o in range(2):

            @pl.when(x == o)
            def _():
                x_own(o, part, 0).start()
                x_own(o, part, 1).start()
                peer_own(o, part).start()
                x_keep(o, part).start()

    def x_near(part):
        for o in range(2):

            @pl.when(x == 1 - o)
            def _():
                x_pass(o, part, peer).wait_recv()
                peer_pass(o, part, core).start()
                x_keep(1 - o, part).wait()

        for near, mine, device in ((1, 2, after), (0, 3, before)):

            @pl.when(x == mine)
            def _():
                x_pass(near, part, device).wait_recv()
                x_pass(near, part, device).start()
                peer_pass(near, part, core).start()

    def x_far(part):
        for far, mine in ((0, 2), (1, 3)):

            @pl.when(x == mine)
            def _():
                x_pass(far, part, peer).wait_recv()
                peer_pass(far, part, core).start()

    def peer_take(part):
        for o in range(2):
            peer_pass(o, part, 1 - core).wait_recv()

    def x_finish():
        for part in range(4):
            for o in range(2):

                @pl.when(x == o)
                def _():
                    x_own(o, part, 0).wait_send()
                    x_own(o, part, 1).wait_send()
                    peer_own(o, part).wait_send()
                    peer_pass(1 - o, part, core).wait_send()

            @pl.when(x >= 2)
            def _():
                x_pass(0, part, peer).wait_send()
                for o in range(2):
                    peer_pass(o, part, core).wait_send()

    def lead_block(s, unit, of_core):
        start = pl.multiple_of((unit // 2) * 256 + of_core * 128 + (unit % 2) * UNIT, UNIT)
        return z.at[pl.ds(start, UNIT), pl.ds(pl.multiple_of(s * 256, 256), 256)]

    def lead_root(unit):
        start = pl.multiple_of((unit // 2) * 256 + core * 128 + (unit % 2) * UNIT, UNIT)
        return z.at[pl.ds(start, UNIT), pl.ds(1024, 256)]

    def row_block(s, t, q):
        return ar.at[s, pl.ds(pl.multiple_of(t * 512 + q * UNIT, UNIT), UNIT)]

    def forward(e, leading):
        code = order[e]
        s = (zz - code % 4 + 4) % 4
        q = (code // 4) % 16
        t = (code // 64) % 4
        root = (code // 256) % 2
        links = code // 512
        flags = [(links // (1 << d)) % 2 == 1 for d in range(4)]
        if leading:
            unit = q * 4 + t
            lead = (q < LEAD) & (unit // 2 <= s)

            @pl.when(lead & (root == 1))
            def _():
                for d in range(4):

                    @pl.when(flags[d])
                    def _():
                        remote(lead_root(unit), lead_block(s, unit, core), ks.at[s, unit, d], kr.at[s, unit], around[d]).start()

            @pl.when(lead & (root == 0))
            def _():
                block = lead_block(s, unit, core)
                remote(block, block, ps.at[s, unit], kr.at[s, unit], peer).wait_recv()
                for d in range(4):

                    @pl.when(flags[d])
                    def _():
                        remote(block, block, ks.at[s, unit, d], kr.at[s, unit], around[d]).start()

                remote(block, block, ps.at[s, unit], pr.at[s, unit], peer).start()

        def pass_row():
            n = q - LEAD
            block = row_block(s, t, n)

            @pl.when(root == 0)
            def _():
                remote(block, block, rs.at[s, t, 0], rr.at[s, t, n], peer).wait_recv()

            for d in range(4):

                @pl.when(flags[d] & ((root == 0) | (n > 0)))
                def _():
                    remote(block, block, rs.at[s, t, d], rr.at[s, t, n], around[d]).start()

        if leading:
            pl.when(q >= LEAD)(pass_row)
        else:
            pass_row()

    x_start(0)

    @pl.when(y == 0)
    def _():
        keep_column.wait()
        for t in range(4):
            (d,) = CHILDREN[t][0, 0]
            block = row_block(zz, t, 0)
            remote(block, block, rs.at[zz, t, d], rr.at[zz, t, 0], around[d]).start()

    x_near(0)
    x_far(0)
    peer_take(0)
    keep_lead = pltpu.make_async_copy(z.at[:, pl.ds(1024, 256)], z.at[:, pl.ds(pl.multiple_of(zz * 256, 256), 256)], ls.at[5])

    @pl.when(y == 0)
    def _():
        keep_lead.start()

    for part in range(1, 4):
        x_start(part)

    for part in range(1, 4):

        @pl.loop((part - 1) * (PREFIX // 3), part * (PREFIX // 3))
        def _(e):
            forward(e, True)

        x_near(part)

    for s in range(4):

        @pl.when(col != s)
        def _():
            for unit in range(2 * s + 2):
                block = lead_block(s, unit, 1 - core)
                remote(block, block, ps.at[s, unit], pr.at[s, unit], peer).wait_recv()

    @pl.when(y == 0)
    def _():
        keep_lead.wait()

    def links_of(s, t):
        index = y * 4 + (zz - s + 4) % 4
        return pick(index, [sum(1 << d for d in CHILDREN[t][a, b]) for a in range(4) for b in range(4)])

    for s in range(4):
        for unit in range(2 * s + 2):
            links = links_of(s, unit % 4)
            block = lead_block(s, unit, core)
            for d in range(4):

                @pl.when((links // (1 << d)) % 2 == 1)
                def _():
                    remote(block, block, ks.at[s, unit, d], kr.at[s, unit], around[d]).wait_send()

            @pl.when(col != s)
            def _():
                remote(block, block, ps.at[s, unit], pr.at[s, unit], peer).wait_send()

    each = (16 * (LEAD + 8) - PREFIX) // 8

    @pl.loop(0, 8)
    def _(step):
        here = pl.multiple_of(step * 128, 128)
        which = step % 2

        def hook(b):
            if b < each:
                forward(PREFIX + each * step + b, False)

        triangle128(
            lambda v: z[pl.ds(pl.multiple_of(here + 8 * v, 8), 8), pl.ds(here, 128)],
            upper,
            inverse.at[pl.ds(pl.multiple_of(which * 128, 128), 128)],
            hook,
        )
        z[pl.ds(here, 128), pl.ds(here, 128)] = upper[...]

        for k in range(4):
            o, mid, end = 256 * k, 256 * k + 128, 256 * k + 256

            @pl.when(step == 2 * k)
            def _():
                if k == 0:
                    for part in range(1, 4):
                        x_far(part)
                    for part in range(1, 4):
                        peer_take(part)
                    x_finish()

                @pl.when(row == k)
                def _():
                    top_ref[...] = z[o:end, 1024:2048]

                corner = product(split(inverse[0:128]), split(z[o:mid, mid:end]))
                z[o:mid, mid:end] = corner
                z[mid:end, mid:end] -= product(split(corner.T), split(corner))

            @pl.when(step == 2 * k + 1)
            def _():
                z[mid:end, o:mid] = jnp.zeros((128, 128), F32)
                low = inverse[128:256]
                high = inverse[0:128]
                side = product(split(z[o:mid, mid:end].T), split(high))
                side = -product(split(low), split(side))
                block = split(
                    jnp.concatenate(
                        [
                            jnp.concatenate([high, jnp.zeros((128, 128), F32)], axis=1),
                            jnp.concatenate([side, low], axis=1),
                        ],
                        axis=0,
                    )
                )
                inverse_high[k], inverse_low[k] = block
                if k < 3:
                    right = product(block, split(z[o:end, end:1024]))
                    z[o:end, end:1024] = right
                    down = split(right.T)
                    z[end:1024, end:1024] -= product(down, split(right))

                for c in range(0, 1024, TILE):
                    cols = slice(1024 + c, 1024 + c + TILE)
                    solved = product(block, split(z[o:end, cols]))
                    z[o:end, cols] = solved
                    if k < 3:
                        z[end:1024, cols] -= product(down, split(solved))

    keep_all = pltpu.make_async_copy(ar, ar_out, ls.at[6])
    keep_all.start()

    @pl.when((col < 4) & (row < 4) & (row >= col))
    def _():
        block = z[pl.ds(pl.multiple_of(jnp.minimum(col, 3) * 256, 256), 256), pl.ds(pl.multiple_of(jnp.minimum(row, 3) * 256, 256), 256)]
        top_ref[:, 0:256] = block.T

    @pl.when((col < 4) & (row < col))
    def _():
        top_ref[:, 0:256] = jnp.zeros((256, 256), F32)

    @pl.when(col < 4)
    def _():
        a = lax.broadcasted_iota(jnp.int32, (1024, 256), 0)
        b = lax.broadcasted_iota(jnp.int32, (1024, 256), 1)
        z[:, 1024:1280] = jnp.where(a == b + col * 256, -1.0, 0.0)

    for k in range(3, -1, -1):
        o, end = 256 * k, 256 * k + 256
        block = inverse_high[k].T, inverse_low[k].T
        side = split(z[o:end, end:1024]) if k < 3 else None
        for c in range(0, 1024, TILE):
            cols = slice(c, c + TILE)
            mine = z[o:end, 1024 + c : 1024 + c + TILE]
            if k < 3:
                mine = mine - product(side, (wh_ref[end:1024, cols], wl_ref[end:1024, cols]))
            wh_ref[o:end, cols], wl_ref[o:end, cols] = split(product(block, split(mine)))

    for s in range(4):
        for t in range(4):
            links = links_of(s, t)
            for d in range(4):

                @pl.when((links // (1 << d)) % 2 == 1)
                def _():
                    block = ar.at[s, pl.ds(t * 512, 512)]
                    remote(block, block, rs.at[s, t, d], rr.at[s, t, 0], around[d]).wait_send()

    keep_all.wait()


def panels(matrix):
    sems = [(4, 2), (2, 4), (2, 4), (2, 4), (4, 8, 4), (4, 8), (4, 8), (4, 8), (4, 4, 4), (4, 4, 8), (7,)]
    vmem = pl.BlockSpec(memory_space=pltpu.VMEM)
    anywhere = pl.BlockSpec(memory_space=pl.ANY)
    return pl.pallas_call(
        panels_kernel,
        out_shape=[
            jax.ShapeDtypeStruct((4, 2048, 256), F32),
            jax.ShapeDtypeStruct((1024, 1024), BF16),
            jax.ShapeDtypeStruct((1024, 1024), BF16),
            jax.ShapeDtypeStruct((256, 1024), F32),
        ],
        in_specs=[anywhere],
        out_specs=[anywhere, vmem, vmem, vmem],
        scratch_shapes=[
            pltpu.VMEM((4, 2048, 256), F32),
            pltpu.VMEM((1024, 2048), F32),
            pltpu.VMEM((256, 128), F32),
            pltpu.VMEM((128, 128), F32),
            pltpu.VMEM((4, 256, 256), BF16),
            pltpu.VMEM((4, 256, 256), BF16),
            pltpu.SMEM((16 * (LEAD + 8),), jnp.int32),
            *[pltpu.SemaphoreType.DMA(s) for s in sems],
        ],
        compiler_params=pltpu.CompilerParams(collective_id=0, has_side_effects=True, vmem_limit_bytes=56 << 20),
        name="panels",
    )(matrix)


def update_kernel(m_ref, a_ref, wh_ref, wl_ref, top_ref, out_ref):
    row, col = lax.axis_index("prow"), lax.axis_index("pcol")
    out_ref[...] = m_ref[...]

    @pl.when(col < 4)
    def _():
        out_ref[:, 0:256] = jnp.zeros((256, 256), F32)

    total = None
    for s in range(4):
        rows = slice(256 * s, 256 * s + 256)
        part = product(split(a_ref[s]), (wh_ref[rows], wl_ref[rows]))
        total = part if total is None else total + part
    out_ref[...] -= total

    @pl.when((pl.program_id(0) == 0) & (row < 4))
    def _():
        out_ref[...] = top_ref[...]


def update(matrix, column, wh, wl, top):
    tile = pl.BlockSpec((256, 1024), lambda i: (i, 0))
    whole = lambda shape: pl.BlockSpec(shape, lambda i: (0, 0))
    return pl.pallas_call(
        update_kernel,
        grid=(8,),
        out_shape=jax.ShapeDtypeStruct((2048, 1024), F32),
        in_specs=[
            tile,
            pl.BlockSpec((4, 256, 256), lambda i: (0, i, 0)),
            whole((1024, 1024)),
            whole((1024, 1024)),
            whole((256, 1024)),
        ],
        out_specs=tile,
        compiler_params=pltpu.CompilerParams(vmem_limit_bytes=60 << 20),
        name="update",
    )(matrix, column, wh, wl, top)


def shards(matrix):
    return update(matrix, *panels(matrix))


def solution(mesh):
    return jax.shard_map(
        shards,
        mesh=mesh,
        in_specs=(P("prow", "pcol"),),
        out_specs=P("prow", "pcol"),
        check_vma=False,
    )
```

time: 1280 us -> 145 us (0.11); the launches traced: 1260 us -> 144 us
  waiting for transfers between devices: 840 us -> 0 us
  other arithmetic: 278 us -> 0 us
  Pallas kernels: 0 us -> 144 us
  matrix products: 62.6 us -> 0 us
  local copies, waits for them, and re-layouts: 61.8 us -> 0 us
  between operations: 19.7 us -> 0.01 us
    psum x12 -> x0, waiting for transfers between devices: 840 us -> none  [spread(): return lax.psum(block, axis)]
    another operation x37 -> x0, other arithmetic: 220 us -> none  [the longest x27 138 us: factor_rows(): triangle = jnp.linalg.cholesky(corner)]
    pallas_call x0 -> x2, Pallas kernels: none -> 144 us  [the longest x1 125 us: panels(): pl.pallas_call(panels_kernel, out_shape=[jax.ShapeDtypeStruct((4, 2048, 2...]
    dot_general x4 -> x0, matrix products: 47.4 us -> none  [subtract(): lax.dot_general(finished, across, (((1,), (1,)), ((), ())), precision=HIG...]
    select_n x16 -> x0, other arithmetic: 37.5 us -> none  [the longest x12 30.5 us: spread(): jnp.where(lax.axis_index(axis) == owner, block, jnp.zeros_like(block))]
    unnamed x25 -> x0, local copies, waits for them, and re-layouts: 17.4 us -> none
    another operation x41 -> x0, local copies, waits for them, and re-layouts: 16.7 us -> none  [the longest x29 16.1 us: factor_rows(): solved = jax.scipy.linalg.solve_triangular(triangle, column.T, lower=True).T]
    scatter x4 -> x0, other arithmetic: 15.8 us -> none  [place_column(): matrix.at[:, at_column:at_column + NB]]
  transfers between devices with their start and end apart: 12 -> 0, of which waited for: 12 -> 0; matrix products, arithmetic and copies ran while one was open for 0% -> 0% of each run, Pallas kernels for 0% -> 0%
where the time goes in v2:
time: 145 us; the launch traced here: 144 us
  Pallas kernels  144 us (99%)
    pallas_call x1, Pallas kernels, panels(): pl.pallas_call(panels_kernel, out_shape=[jax.ShapeDtypeStruct((4, 2048, 2...  125 us
    pallas_call x1, Pallas kernels, update(): pl.pallas_call(update_kernel, grid=(8,), out_shape=jax.ShapeDtypeStruct((...  19.2 us

profile of v2, /device:TPU:22, one launch (start us, length us, event | category | flops | bytes accessed | tf_op | source)
XLA Modules:
  0.0 143.9 jit_solution(2773771356878555248)
XLA Ops:
  0.0 124.7 %panels.1 = (f32[4,2048,256]{2,1,0:T(8,128)}, bf16[1024,1024]{1,0:T(8,128)(2,1)}, bf16[1024,1024]{1,0:T(8,128)(2,1)}, f32[256,1024]{1,0:T(8,128)}) custom-call(f32[2048,1024]{1,0:T(8,128)} %m_ref.1), custom_call_target="tpu_custom_call" | custom-call | tf_op jit(solution)/shard_map/panels/pallas_call | solution.py:529
  124.7 19.2 %update.1 = f32[2048,1024]{1,0:T(8,128)} custom-call(f32[2048,1024]{1,0:T(8,128)} %m_ref.1, f32[4,2048,256]{2,1,0:T(8,128)} %get-tuple-element.9.a_ref, bf16[1024,1024]{1,0:T(8,128)(2,1)} %get-tuple-element.10.wh_ref, bf16[1024,1024]{1,0:T(8,128)(2,1)} %get-tuple-element.11.wl_ref, f32[256,1024]{1,0:T(8,128)} %get-tuple-element.12.top_ref), custom_call_target="tpu_custom_call" | custom-call | tf_op jit(solution)/shard_map/update/pallas_call | solution.py:577

commit v3 on v2

--- a/solution.py
+++ b/solution.py
@@ -33,49 +33,68 @@
 
 CHILDREN = tree_children()
 UNIT = 64
+ROWS = 128
+COPIES = 512 // ROWS
 LEAD = 2
 
-PREFIX = 48
+PREFIX = 32
+EARLY = 1
 ORDER = (
     (
-        8, 72, 136, 200, 73, 203, 74, 202, 0, 64, 128, 192, 4, 68, 132, 196, 201, 75, 9, 137,
-        11, 139, 65, 195, 69, 199, 10, 138, 66, 194, 70, 198, 193, 67, 129, 131, 1, 3, 197, 71,
-        5, 133, 7, 135, 130, 2, 6, 134, 12, 76, 140, 204, 16, 80, 144, 208, 20, 84, 148, 212,
-        24, 88, 152, 216, 28, 92, 156, 220, 32, 96, 160, 224, 36, 100, 164, 228, 77, 207, 81, 211,
-        85, 215, 89, 219, 93, 223, 13, 141, 15, 143, 97, 227, 101, 231, 17, 145, 19, 147, 78, 206,
-        82, 210, 149, 23, 21, 151, 86, 214, 14, 90, 218, 142, 153, 27, 94, 222, 25, 98, 226, 155,
-        157, 31, 102, 230, 18, 205, 79, 146, 161, 35, 209, 83, 29, 159, 213, 87, 165, 39, 217, 91,
-        22, 150, 33, 163, 221, 95, 225, 99, 229, 103, 26, 154, 37, 167, 30, 158, 34, 162, 38, 166,
-    ),
-    (
-        136, 137, 139, 73, 203, 8, 202, 72, 200, 74, 138, 128, 132, 201, 9, 11, 75, 129, 131, 65,
-        195, 133, 135, 69, 10, 199, 64, 66, 194, 0, 192, 130, 4, 198, 68, 70, 196, 134, 193, 1,
-        3, 67, 197, 71, 5, 7, 2, 6, 140, 144, 148, 141, 143, 152, 145, 147, 156, 149, 12, 151,
-        160, 142, 153, 16, 164, 155, 157, 20, 146, 161, 15, 77, 207, 159, 165, 13, 19, 150, 81, 211,
-        163, 78, 24, 204, 85, 215, 167, 208, 82, 154, 14, 17, 23, 76, 79, 89, 219, 158, 28, 212,
-        86, 80, 93, 223, 83, 162, 18, 21, 27, 84, 32, 97, 227, 216, 90, 166, 88, 231, 22, 101,
-        87, 92, 220, 94, 206, 96, 31, 36, 25, 210, 100, 205, 224, 98, 214, 26, 91, 35, 218, 209,
-        222, 213, 228, 102, 29, 226, 217, 95, 39, 30, 230, 221, 33, 99, 225, 229, 34, 103, 37, 38,
-    ),
-    (
-        8, 136, 137, 11, 9, 73, 139, 203, 74, 202, 72, 200, 10, 138, 0, 128, 4, 132, 201, 75,
-        129, 3, 1, 65, 131, 195, 133, 7, 5, 69, 135, 199, 194, 130, 66, 64, 2, 192, 198, 70,
-        68, 196, 6, 134, 67, 193, 71, 197, 12, 140, 16, 144, 15, 141, 20, 148, 13, 143, 19, 145,
-        24, 152, 149, 23, 14, 142, 17, 147, 28, 156, 18, 146, 27, 153, 21, 151, 32, 160, 22, 150,
-        31, 157, 36, 164, 25, 155, 26, 154, 35, 161, 207, 77, 29, 159, 39, 165, 211, 81, 30, 158,
-        33, 163, 76, 204, 34, 162, 215, 85, 37, 167, 219, 89, 80, 38, 208, 166, 223, 93, 84, 212,
-        227, 97, 88, 216, 92, 220, 231, 101, 78, 206, 96, 224, 82, 210, 100, 228, 205, 79, 86, 214,
-        90, 218, 209, 83, 94, 222, 213, 87, 98, 226, 217, 91, 102, 230, 221, 95, 225, 99, 229, 103,
-    ),
-    (
-        8, 9, 11, 73, 203, 136, 74, 72, 200, 10, 202, 0, 4, 75, 137, 139, 1, 3, 201, 65,
-        195, 5, 7, 69, 138, 199, 64, 2, 128, 66, 192, 194, 132, 70, 68, 6, 196, 198, 129, 67,
-        193, 131, 71, 133, 197, 135, 130, 134, 12, 16, 20, 13, 15, 24, 17, 19, 28, 23, 140, 21,
-        32, 14, 27, 144, 36, 25, 31, 148, 18, 35, 141, 77, 207, 29, 39, 143, 145, 22, 81, 211,
-        33, 206, 152, 76, 85, 215, 37, 80, 210, 26, 142, 147, 149, 204, 205, 89, 219, 30, 156, 84,
-        214, 208, 93, 223, 209, 34, 146, 151, 153, 212, 160, 97, 227, 88, 218, 38, 216, 101, 150, 231,
-        213, 92, 220, 222, 78, 224, 157, 164, 155, 82, 228, 79, 96, 226, 86, 154, 217, 161, 90, 83,
-        94, 87, 100, 230, 159, 98, 91, 221, 165, 158, 102, 95, 163, 225, 99, 103, 162, 229, 167, 166,
+        0, 64, 128, 192, 4, 68, 132, 196, 65, 195, 69, 199, 66, 194, 70, 198, 193, 67, 129, 131,
+        1, 3, 197, 71, 5, 133, 7, 135, 130, 2, 6, 134, 8, 72, 136, 200, 73, 203, 12, 76,
+        140, 204, 16, 80, 144, 208, 20, 84, 148, 212, 74, 202, 77, 207, 81, 211, 9, 11, 137, 139,
+        85, 215, 201, 75, 10, 138, 78, 206, 13, 15, 82, 210, 141, 143, 86, 214, 17, 205, 79, 19,
+        147, 145, 209, 83, 21, 213, 87, 14, 23, 151, 149, 142, 18, 146, 22, 150,
+    ),
+    (
+        128, 132, 129, 131, 65, 195, 133, 135, 69, 199, 0, 64, 66, 194, 192, 130, 4, 198, 68, 70,
+        196, 134, 193, 1, 3, 67, 197, 71, 5, 7, 2, 6, 136, 73, 203, 137, 139, 140, 8, 72,
+        200, 74, 144, 138, 148, 141, 143, 11, 9, 202, 147, 75, 145, 12, 77, 207, 151, 10, 149, 142,
+        16, 201, 81, 211, 204, 78, 146, 15, 13, 20, 85, 215, 76, 150, 208, 82, 79, 19, 206, 80,
+        210, 84, 14, 17, 212, 86, 214, 205, 83, 23, 209, 18, 87, 21, 213, 22,
+    ),
+    (
+        0, 128, 4, 132, 129, 3, 1, 65, 131, 195, 133, 7, 5, 69, 135, 199, 194, 130, 66, 64,
+        2, 192, 198, 70, 68, 196, 6, 134, 67, 193, 71, 197, 8, 136, 203, 11, 73, 137, 9, 139,
+        12, 72, 200, 140, 10, 138, 16, 144, 15, 141, 13, 20, 148, 19, 145, 143, 14, 202, 142, 74,
+        17, 149, 23, 147, 18, 146, 207, 21, 77, 151, 201, 75, 211, 22, 150, 81, 76, 215, 204, 85,
+        78, 80, 208, 206, 82, 84, 212, 210, 86, 205, 79, 214, 209, 83, 213, 87,
+    ),
+    (
+        0, 4, 1, 3, 65, 195, 5, 7, 69, 199, 128, 64, 2, 66, 192, 194, 132, 70, 68, 6,
+        196, 198, 129, 67, 193, 131, 71, 133, 197, 135, 130, 134, 8, 73, 203, 9, 11, 12, 72, 200,
+        202, 136, 10, 16, 13, 15, 20, 137, 201, 17, 74, 139, 19, 14, 21, 77, 207, 140, 23, 138,
+        76, 206, 144, 75, 18, 81, 211, 141, 148, 204, 22, 85, 215, 205, 80, 210, 143, 145, 208, 78,
+        212, 82, 214, 84, 142, 79, 209, 86, 149, 147, 83, 213, 87, 146, 151, 150,
+    ),
+    (
+        0, 64, 128, 192, 4, 68, 132, 196, 65, 195, 69, 199, 66, 194, 70, 198, 193, 67, 129, 131,
+        1, 3, 197, 71, 5, 133, 7, 135, 130, 2, 6, 134, 8, 72, 136, 200, 73, 203, 12, 76,
+        140, 204, 16, 80, 144, 208, 20, 84, 148, 212, 74, 202, 77, 207, 81, 211, 9, 11, 137, 139,
+        85, 215, 201, 75, 10, 138, 78, 206, 13, 15, 82, 210, 141, 143, 86, 214, 17, 205, 79, 147,
+        19, 145, 209, 83, 14, 21, 213, 87, 23, 151, 149, 142, 18, 146, 22, 150,
+    ),
+    (
+        128, 132, 129, 131, 65, 195, 133, 135, 69, 199, 0, 64, 66, 194, 192, 130, 4, 198, 68, 70,
+        196, 134, 193, 1, 3, 67, 197, 71, 5, 7, 2, 6, 136, 73, 203, 137, 139, 140, 8, 72,
+        200, 74, 144, 138, 148, 141, 143, 11, 9, 202, 147, 75, 145, 12, 77, 207, 151, 149, 10, 142,
+        16, 201, 81, 211, 204, 78, 146, 15, 13, 20, 85, 215, 76, 150, 208, 82, 79, 19, 206, 80,
+        210, 84, 14, 17, 212, 86, 214, 205, 83, 23, 209, 18, 87, 21, 213, 22,
+    ),
+    (
+        0, 128, 4, 132, 129, 3, 1, 65, 131, 195, 133, 7, 5, 69, 135, 199, 194, 130, 66, 64,
+        2, 192, 198, 70, 68, 196, 6, 134, 67, 193, 71, 197, 8, 136, 203, 11, 73, 137, 9, 139,
+        12, 72, 200, 140, 10, 138, 16, 144, 15, 141, 13, 20, 148, 19, 145, 143, 14, 202, 142, 74,
+        17, 149, 23, 147, 18, 146, 207, 21, 77, 151, 201, 75, 211, 22, 150, 81, 76, 215, 204, 85,
+        78, 80, 208, 206, 82, 84, 212, 210, 86, 205, 79, 214, 209, 83, 213, 87,
+    ),
+    (
+        0, 4, 1, 3, 65, 195, 5, 7, 69, 199, 128, 64, 2, 66, 192, 194, 132, 70, 68, 6,
+        196, 198, 129, 67, 193, 131, 71, 133, 197, 135, 130, 134, 8, 73, 203, 9, 11, 12, 72, 200,
+        202, 136, 10, 16, 13, 15, 20, 137, 201, 17, 74, 139, 19, 14, 21, 77, 207, 140, 23, 138,
+        76, 206, 144, 75, 18, 81, 211, 141, 148, 204, 22, 85, 215, 205, 80, 210, 143, 145, 208, 78,
+        212, 82, 214, 84, 142, 79, 209, 86, 149, 147, 83, 213, 87, 146, 151, 150,
     ),
 )
 
@@ -178,10 +197,12 @@
 
 
 TILE = 512
+EXTRA = 2
+HOOKS = (1, 4, 6, 8, 10, 13, 15)
 
 
 def panels_kernel(
-    k_ref, ar_out, wh_ref, wl_ref, top_ref, ar, z, inverse, upper, inverse_high, inverse_low, order, xs, xr, cs, cr, ks, kr, ps, pr, rs, rr, ls
+    k_ref, m, ar, wh_ref, wl_ref, top_ref, z, inverse, upper, inverse_high, inverse_low, order, xs, xr, cs, cr, ks, kr, ps, pr, rs, rr, ls
 ):
     x, core, y, zz = place()
     row, col = x * 2 + core, y * 4 + zz
@@ -190,44 +211,54 @@
         return (px * 2 + pcore, py * 4 + pz)
 
     peer = at(x, 1 - core, y, zz)
-    after, before = at((x + 1) % 4, core, y, zz), at((x + 3) % 4, core, y, zz)
+    after, before, across = (at((x + d) % 4, core, y, zz) for d in (1, 3, 2))
     around = [at(x, core, (y + dy + 4) % 4, (zz + dz + 4) % 4) for dy, dz in TURNS]
     barrier = pltpu.get_barrier_semaphore()
-    for device in [peer, after, before, *around]:
+    for device in [peer, after, before, across, *around]:
         pl.semaphore_signal(barrier, inc=1, device_id=device, device_id_type=MESH)
 
+    def top_rows(o, of_core, part):
+        return z.at[pl.ds(pl.multiple_of(o * 512 + of_core * 256, 256), 256), pl.ds(1024 + 256 * part, 256)]
+
+    def own_top(part):
+        return k_ref.at[pl.ds(0, 256), pl.ds(256 * part, 256)]
+
+    def x_keep(o, part):
+        return pltpu.make_async_copy(own_top(part), top_rows(o, core, part), ls.at[part])
+
+    for o in range(2):
+
+        @pl.when(x == o)
+        def _():
+            for part in range(4):
+                x_keep(o, part).start()
+
     keep_column = pltpu.make_async_copy(k_ref.at[:, pl.ds(0, 256)], ar.at[zz], ls.at[4])
+    keep_block = pltpu.make_async_copy(k_ref, m, ls.at[6])
 
     @pl.when(y == 0)
     def _():
         keep_column.start()
 
-    for e in range(16 * (LEAD + 8)):
-        order[e] = pick(y, [packed(i, ORDER[i][e]) for i in range(4)])
-
-    pl.semaphore_wait(barrier, 7)
+    for e in range(16 * (LEAD + COPIES)):
+        order[e] = pick(y + 4 * (x // 2), [packed(i % 4, ORDER[i][e]) for i in range(8)])
+
+    pl.semaphore_wait(barrier, 8)
 
     def remote(src, dst, ssem, rsem, device):
         return pltpu.make_async_remote_copy(src, dst, ssem, rsem, device_id=device, device_id_type=MESH)
 
-    def top_rows(o, of_core, part):
-        return z.at[pl.ds(pl.multiple_of(o * 512 + of_core * 256, 256), 256), pl.ds(1024 + 256 * part, 256)]
-
-    def own_top(part):
-        return k_ref.at[pl.ds(0, 256), pl.ds(256 * part, 256)]
-
     def x_own(o, part, i):
-        return remote(own_top(part), top_rows(o, core, part), xs.at[part, i], xr.at[o, part], (after, before)[i])
+        block = top_rows(o, core, part)
+        return remote(block, block, xs.at[part, i], xr.at[o, part], (after, before, across)[i])
 
     def x_pass(o, part, device):
         block = top_rows(o, core, part)
         return remote(block, block, xs.at[part, 0], xr.at[o, part], device)
 
-    def x_keep(o, part):
-        return pltpu.make_async_copy(own_top(part), top_rows(o, core, part), ls.at[part])
-
     def peer_own(o, part):
-        return remote(own_top(part), top_rows(o, core, part), cs.at[o, part], cr.at[o, part], peer)
+        block = top_rows(o, core, part)
+        return remote(block, block, cs.at[o, part], cr.at[o, part], peer)
 
     def peer_pass(o, part, of_core):
         block = top_rows(o, of_core, part)
@@ -238,10 +269,12 @@
 
             @pl.when(x == o)
             def _():
+                x_keep(o, part).wait()
                 x_own(o, part, 0).start()
                 x_own(o, part, 1).start()
+                if part == 0:
+                    x_own(o, part, 2).start()
                 peer_own(o, part).start()
-                x_keep(o, part).start()
 
     def x_near(part):
         for o in range(2):
@@ -250,14 +283,14 @@
             def _():
                 x_pass(o, part, peer).wait_recv()
                 peer_pass(o, part, core).start()
-                x_keep(1 - o, part).wait()
 
         for near, mine, device in ((1, 2, after), (0, 3, before)):
 
             @pl.when(x == mine)
             def _():
                 x_pass(near, part, device).wait_recv()
-                x_pass(near, part, device).start()
+                if part > 0:
+                    x_pass(near, part, device).start()
                 peer_pass(near, part, core).start()
 
     def x_far(part):
@@ -280,12 +313,15 @@
                 def _():
                     x_own(o, part, 0).wait_send()
                     x_own(o, part, 1).wait_send()
+                    if part == 0:
+                        x_own(o, part, 2).wait_send()
                     peer_own(o, part).wait_send()
                     peer_pass(1 - o, part, core).wait_send()
 
             @pl.when(x >= 2)
             def _():
-                x_pass(0, part, peer).wait_send()
+                if part > 0:
+                    x_pass(0, part, peer).wait_send()
                 for o in range(2):
                     peer_pass(o, part, core).wait_send()
 
@@ -298,7 +334,7 @@
         return z.at[pl.ds(start, UNIT), pl.ds(1024, 256)]
 
     def row_block(s, t, q):
-        return ar.at[s, pl.ds(pl.multiple_of(t * 512 + q * UNIT, UNIT), UNIT)]
+        return ar.at[s, pl.ds(pl.multiple_of(t * 512 + q * ROWS, ROWS), ROWS)]
 
     def forward(e, leading):
         code = order[e]
@@ -342,7 +378,7 @@
 
             for d in range(4):
 
-                @pl.when(flags[d] & ((root == 0) | (n > 0)))
+                @pl.when(flags[d] & ((root == 0) | (n >= EARLY)))
                 def _():
                     remote(block, block, rs.at[s, t, d], rr.at[s, t, n], around[d]).start()
 
@@ -351,23 +387,25 @@
         else:
             pass_row()
 
+    keep_lead = pltpu.make_async_copy(z.at[:, pl.ds(1024, 256)], z.at[:, pl.ds(pl.multiple_of(zz * 256, 256), 256)], ls.at[5])
+
+    def x_first():
+        x_near(0)
+        x_far(0)
+        peer_take(0)
+
     x_start(0)
 
     @pl.when(y == 0)
     def _():
         keep_column.wait()
-        for t in range(4):
-            (d,) = CHILDREN[t][0, 0]
-            block = row_block(zz, t, 0)
-            remote(block, block, rs.at[zz, t, d], rr.at[zz, t, 0], around[d]).start()
-
-    x_near(0)
-    x_far(0)
-    peer_take(0)
-    keep_lead = pltpu.make_async_copy(z.at[:, pl.ds(1024, 256)], z.at[:, pl.ds(pl.multiple_of(zz * 256, 256), 256)], ls.at[5])
-
-    @pl.when(y == 0)
-    def _():
+        for q in range(EARLY):
+            for t in range(4):
+                (d,) = CHILDREN[t][0, 0]
+                block = row_block(zz, t, q)
+                remote(block, block, rs.at[zz, t, d], rr.at[zz, t, q], around[d]).start()
+
+        x_first()
         keep_lead.start()
 
     for part in range(1, 4):
@@ -375,10 +413,12 @@
 
     for part in range(1, 4):
 
-        @pl.loop((part - 1) * (PREFIX // 3), part * (PREFIX // 3))
+        @pl.loop(PREFIX * (part - 1) // 3, PREFIX * part // 3)
         def _(e):
             forward(e, True)
 
+        if part == 1:
+            pl.when(y != 0)(x_first)
         x_near(part)
 
     for s in range(4):
@@ -393,6 +433,8 @@
     def _():
         keep_lead.wait()
 
+    keep_block.start()
+
     def links_of(s, t):
         index = y * 4 + (zz - s + 4) % 4
         return pick(index, [sum(1 << d for d in CHILDREN[t][a, b]) for a in range(4) for b in range(4)])
@@ -411,7 +453,6 @@
             def _():
                 remote(block, block, ps.at[s, unit], pr.at[s, unit], peer).wait_send()
 
-    each = (16 * (LEAD + 8) - PREFIX) // 8
 
     @pl.loop(0, 8)
     def _(step):
@@ -419,8 +460,8 @@
         which = step % 2
 
         def hook(b):
-            if b < each:
-                forward(PREFIX + each * step + b, False)
+            if b in HOOKS:
+                forward(PREFIX + len(HOOKS) * step + EXTRA * (step // 2) + HOOKS.index(b), False)
 
         triangle128(
             lambda v: z[pl.ds(pl.multiple_of(here + 8 * v, 8), 8), pl.ds(here, 128)],
@@ -435,17 +476,6 @@
 
             @pl.when(step == 2 * k)
             def _():
-                if k == 0:
-                    for part in range(1, 4):
-                        x_far(part)
-                    for part in range(1, 4):
-                        peer_take(part)
-                    x_finish()
-
-                @pl.when(row == k)
-                def _():
-                    top_ref[...] = z[o:end, 1024:2048]
-
                 corner = product(split(inverse[0:128]), split(z[o:mid, mid:end]))
                 z[o:mid, mid:end] = corner
                 z[mid:end, mid:end] -= product(split(corner.T), split(corner))
@@ -453,6 +483,12 @@
             @pl.when(step == 2 * k + 1)
             def _():
                 z[mid:end, o:mid] = jnp.zeros((128, 128), F32)
+                spare = iter(range(PREFIX + (2 * len(HOOKS) + EXTRA) * k + 2 * len(HOOKS), PREFIX + (2 * len(HOOKS) + EXTRA) * (k + 1)))
+
+                def between(count):
+                    for e in [e for _, e in zip(range(count), spare)]:
+                        forward(jnp.int32(e), False)
+
                 low = inverse[128:256]
                 high = inverse[0:128]
                 side = product(split(z[o:mid, mid:end].T), split(high))
@@ -467,11 +503,24 @@
                     )
                 )
                 inverse_high[k], inverse_low[k] = block
+                between(1)
                 if k < 3:
                     right = product(block, split(z[o:end, end:1024]))
                     z[o:end, end:1024] = right
                     down = split(right.T)
                     z[end:1024, end:1024] -= product(down, split(right))
+                between(1)
+
+                if k == 0:
+                    for part in range(1, 4):
+                        x_far(part)
+                    for part in range(1, 4):
+                        peer_take(part)
+                    x_finish()
+
+                @pl.when(row == k)
+                def _():
+                    top_ref[...] = z[o:end, 1024:2048]
 
                 for c in range(0, 1024, TILE):
                     cols = slice(1024 + c, 1024 + c + TILE)
@@ -479,9 +528,7 @@
                     z[o:end, cols] = solved
                     if k < 3:
                         z[end:1024, cols] -= product(down, split(solved))
-
-    keep_all = pltpu.make_async_copy(ar, ar_out, ls.at[6])
-    keep_all.start()
+                    between(1 if c == 0 else EXTRA)
 
     @pl.when((col < 4) & (row < 4) & (row >= col))
     def _():
@@ -509,6 +556,16 @@
                 mine = mine - product(side, (wh_ref[end:1024, cols], wl_ref[end:1024, cols]))
             wh_ref[o:end, cols], wl_ref[o:end, cols] = split(product(block, split(mine)))
 
+    keep_block.wait()
+
+    @pl.when(col < 4)
+    def _():
+        m[:, 0:256] = jnp.zeros((2048, 256), F32)
+
+    @pl.loop(PREFIX + 8 * len(HOOKS) + 4 * EXTRA, 16 * (LEAD + COPIES))
+    def _(e):
+        forward(e, False)
+
     for s in range(4):
         for t in range(4):
             links = links_of(s, t)
@@ -519,80 +576,56 @@
                     block = ar.at[s, pl.ds(t * 512, 512)]
                     remote(block, block, rs.at[s, t, d], rr.at[s, t, 0], around[d]).wait_send()
 
-    keep_all.wait()
-
 
 def panels(matrix):
-    sems = [(4, 2), (2, 4), (2, 4), (2, 4), (4, 8, 4), (4, 8), (4, 8), (4, 8), (4, 4, 4), (4, 4, 8), (7,)]
-    vmem = pl.BlockSpec(memory_space=pltpu.VMEM)
-    anywhere = pl.BlockSpec(memory_space=pl.ANY)
+    sems = [(4, 3), (2, 4), (2, 4), (2, 4), (4, 8, 4), (4, 8), (4, 8), (4, 8), (4, 4, 4), (4, 4, COPIES), (7,)]
     return pl.pallas_call(
         panels_kernel,
         out_shape=[
+            jax.ShapeDtypeStruct((2048, 1024), F32),
             jax.ShapeDtypeStruct((4, 2048, 256), F32),
             jax.ShapeDtypeStruct((1024, 1024), BF16),
             jax.ShapeDtypeStruct((1024, 1024), BF16),
             jax.ShapeDtypeStruct((256, 1024), F32),
         ],
-        in_specs=[anywhere],
-        out_specs=[anywhere, vmem, vmem, vmem],
+        in_specs=[pl.BlockSpec(memory_space=pl.ANY)],
+        out_specs=[pl.BlockSpec(memory_space=pltpu.VMEM)] * 5,
         scratch_shapes=[
-            pltpu.VMEM((4, 2048, 256), F32),
             pltpu.VMEM((1024, 2048), F32),
             pltpu.VMEM((256, 128), F32),
             pltpu.VMEM((128, 128), F32),
             pltpu.VMEM((4, 256, 256), BF16),
             pltpu.VMEM((4, 256, 256), BF16),
-            pltpu.SMEM((16 * (LEAD + 8),), jnp.int32),
+            pltpu.SMEM((16 * (LEAD + COPIES),), jnp.int32),
             *[pltpu.SemaphoreType.DMA(s) for s in sems],
         ],
-        compiler_params=pltpu.CompilerParams(collective_id=0, has_side_effects=True, vmem_limit_bytes=56 << 20),
+        compiler_params=pltpu.CompilerParams(collective_id=0, has_side_effects=True, vmem_limit_bytes=26 << 20),
         name="panels",
     )(matrix)
 
 
-def update_kernel(m_ref, a_ref, wh_ref, wl_ref, top_ref, out_ref):
-    row, col = lax.axis_index("prow"), lax.axis_index("pcol")
-    out_ref[...] = m_ref[...]
-
-    @pl.when(col < 4)
-    def _():
-        out_ref[:, 0:256] = jnp.zeros((256, 256), F32)
-
-    total = None
-    for s in range(4):
-        rows = slice(256 * s, 256 * s + 256)
-        part = product(split(a_ref[s]), (wh_ref[rows], wl_ref[rows]))
-        total = part if total is None else total + part
-    out_ref[...] -= total
-
-    @pl.when((pl.program_id(0) == 0) & (row < 4))
-    def _():
-        out_ref[...] = top_ref[...]
-
-
-def update(matrix, column, wh, wl, top):
-    tile = pl.BlockSpec((256, 1024), lambda i: (i, 0))
-    whole = lambda shape: pl.BlockSpec(shape, lambda i: (0, 0))
+def update_kernel(m, ar, wh, wl, top, out):
+    i = pl.program_id(0)
+    rows = pl.ds(pl.multiple_of(i * 256, 256), 256)
+    total = m[rows]
+    left = split(jnp.concatenate([ar[s, rows] for s in range(4)], axis=1))
+    out[...] = total - product(left, (wh[...], wl[...]))
+
+    @pl.when((i == 0) & (lax.axis_index("prow") < 4))
+    def _():
+        out[...] = top[...]
+
+
+def shards(matrix):
     return pl.pallas_call(
         update_kernel,
         grid=(8,),
         out_shape=jax.ShapeDtypeStruct((2048, 1024), F32),
-        in_specs=[
-            tile,
-            pl.BlockSpec((4, 256, 256), lambda i: (0, i, 0)),
-            whole((1024, 1024)),
-            whole((1024, 1024)),
-            whole((256, 1024)),
-        ],
-        out_specs=tile,
-        compiler_params=pltpu.CompilerParams(vmem_limit_bytes=60 << 20),
+        in_specs=[pl.BlockSpec(memory_space=pltpu.VMEM)] * 5,
+        out_specs=pl.BlockSpec((256, 1024), lambda i: (i, 0)),
+        compiler_params=pltpu.CompilerParams(vmem_limit_bytes=20 << 20),
         name="update",
-    )(matrix, column, wh, wl, top)
-
-
-def shards(matrix):
-    return update(matrix, *panels(matrix))
+    )(*panels(matrix))
 
 
 def solution(mesh):

time: 145 us -> 137 us (0.945)
  Pallas kernels: 144 us -> 136 us
    pallas_call x2, Pallas kernels: 144 us -> 136 us  [the longest x1 121 us: panels(): pl.pallas_call(panels_kernel, out_shape=[jax.ShapeDtypeStruct((2048, 1024...]
where the time goes in v3:
time: 137 us; the launch traced here: 136 us
  Pallas kernels  136 us (99%)
    pallas_call x1, Pallas kernels, panels(): pl.pallas_call(panels_kernel, out_shape=[jax.ShapeDtypeStruct((2048, 1024...  121 us
    pallas_call x1, Pallas kernels, shards(): pl.pallas_call(update_kernel, grid=(8,), out_shape=jax.ShapeDtypeStruct((...  15.4 us

profile of v3, /device:TPU:22, one launch (start us, length us, event | category | flops | bytes accessed | tf_op | source)
XLA Modules:
  0.0 136.5 jit_solution(9620374686089100723)
XLA Ops:
  0.0 121.1 %panels.1 = (f32[2048,1024]{1,0:T(8,128)S(1)}, f32[4,2048,256]{2,1,0:T(8,128)S(1)}, bf16[1024,1024]{1,0:T(8,128)(2,1)S(1)}, bf16[1024,1024]{1,0:T(8,128)(2,1)S(1)}, f32[256,1024]{1,0:T(8,128)S(1)}) custom-call(f32[2048,1024]{1,0:T(8,128)} %k_ref.1), custom_call_target="tpu_custom_call" | custom-call | tf_op jit(solution)/shard_map/panels/pallas_call | solution.py:582
  121.1 15.4 %update.1 = f32[2048,1024]{1,0:T(8,128)} custom-call(f32[2048,1024]{1,0:T(8,128)S(1)} %get-tuple-element.10.m, f32[4,2048,256]{2,1,0:T(8,128)S(1)} %get-tuple-element.11.ar, bf16[1024,1024]{1,0:T(8,128)(2,1)S(1)} %get-tuple-element.12.wh, bf16[1024,1024]{1,0:T(8,128)(2,1)S(1)} %get-tuple-element.13.wl, f32[256,1024]{1,0:T(8,128)S(1)} %get-tuple-element.14.top), custom_call_target="tpu_custom_call" | custom-call | tf_op jit(solution)/shard_map/update/pallas_call | solution.py:620

commit v4 on v3

--- a/solution.py
+++ b/solution.py
@@ -38,63 +38,63 @@
 LEAD = 2
 
 PREFIX = 32
-EARLY = 1
+EARLY = 2
 ORDER = (
     (
         0, 64, 128, 192, 4, 68, 132, 196, 65, 195, 69, 199, 66, 194, 70, 198, 193, 67, 129, 131,
-        1, 3, 197, 71, 5, 133, 7, 135, 130, 2, 6, 134, 8, 72, 136, 200, 73, 203, 12, 76,
-        140, 204, 16, 80, 144, 208, 20, 84, 148, 212, 74, 202, 77, 207, 81, 211, 9, 11, 137, 139,
-        85, 215, 201, 75, 10, 138, 78, 206, 13, 15, 82, 210, 141, 143, 86, 214, 17, 205, 79, 19,
-        147, 145, 209, 83, 21, 213, 87, 14, 23, 151, 149, 142, 18, 146, 22, 150,
+        1, 3, 197, 71, 5, 133, 7, 135, 130, 2, 6, 134, 8, 72, 136, 200, 12, 76, 140, 204,
+        73, 203, 77, 207, 16, 80, 144, 208, 20, 84, 148, 212, 74, 202, 78, 206, 81, 211, 9, 11,
+        137, 139, 85, 215, 201, 75, 13, 15, 141, 143, 205, 79, 10, 82, 210, 138, 14, 86, 214, 142,
+        209, 83, 17, 147, 213, 87, 19, 145, 21, 151, 23, 149, 18, 146, 22, 150,
     ),
     (
         128, 132, 129, 131, 65, 195, 133, 135, 69, 199, 0, 64, 66, 194, 192, 130, 4, 198, 68, 70,
-        196, 134, 193, 1, 3, 67, 197, 71, 5, 7, 2, 6, 136, 73, 203, 137, 139, 140, 8, 72,
-        200, 74, 144, 138, 148, 141, 143, 11, 9, 202, 147, 75, 145, 12, 77, 207, 151, 10, 149, 142,
-        16, 201, 81, 211, 204, 78, 146, 15, 13, 20, 85, 215, 76, 150, 208, 82, 79, 19, 206, 80,
-        210, 84, 14, 17, 212, 86, 214, 205, 83, 23, 209, 18, 87, 21, 213, 22,
+        196, 134, 193, 1, 3, 67, 197, 71, 5, 7, 2, 6, 136, 140, 73, 203, 137, 139, 141, 143,
+        8, 77, 207, 72, 12, 200, 74, 144, 11, 138, 148, 142, 204, 78, 9, 76, 202, 15, 206, 147,
+        10, 75, 13, 145, 151, 81, 211, 201, 149, 14, 16, 79, 205, 85, 215, 146, 20, 208, 82, 210,
+        19, 80, 150, 214, 86, 212, 17, 23, 84, 18, 83, 209, 213, 87, 21, 22,
     ),
     (
         0, 128, 4, 132, 129, 3, 1, 65, 131, 195, 133, 7, 5, 69, 135, 199, 194, 130, 66, 64,
-        2, 192, 198, 70, 68, 196, 6, 134, 67, 193, 71, 197, 8, 136, 203, 11, 73, 137, 9, 139,
-        12, 72, 200, 140, 10, 138, 16, 144, 15, 141, 13, 20, 148, 19, 145, 143, 14, 202, 142, 74,
-        17, 149, 23, 147, 18, 146, 207, 21, 77, 151, 201, 75, 211, 22, 150, 81, 76, 215, 204, 85,
-        78, 80, 208, 206, 82, 84, 212, 210, 86, 205, 79, 214, 209, 83, 213, 87,
+        2, 192, 198, 70, 68, 196, 6, 134, 67, 193, 71, 197, 8, 136, 12, 140, 11, 137, 203, 73,
+        9, 15, 141, 10, 139, 13, 138, 143, 200, 72, 207, 77, 14, 142, 16, 144, 76, 204, 20, 148,
+        19, 145, 74, 202, 149, 23, 17, 206, 78, 18, 147, 75, 146, 201, 21, 211, 81, 151, 22, 150,
+        205, 79, 215, 85, 80, 208, 82, 210, 84, 212, 86, 214, 209, 83, 213, 87,
     ),
     (
         0, 4, 1, 3, 65, 195, 5, 7, 69, 199, 128, 64, 2, 66, 192, 194, 132, 70, 68, 6,
-        196, 198, 129, 67, 193, 131, 71, 133, 197, 135, 130, 134, 8, 73, 203, 9, 11, 12, 72, 200,
-        202, 136, 10, 16, 13, 15, 20, 137, 201, 17, 74, 139, 19, 14, 21, 77, 207, 140, 23, 138,
-        76, 206, 144, 75, 18, 81, 211, 141, 148, 204, 22, 85, 215, 205, 80, 210, 143, 145, 208, 78,
-        212, 82, 214, 84, 142, 79, 209, 86, 149, 147, 83, 213, 87, 146, 151, 150,
+        196, 198, 129, 67, 193, 131, 71, 133, 197, 135, 130, 134, 8, 12, 73, 203, 9, 11, 13, 15,
+        77, 207, 136, 200, 72, 202, 10, 140, 16, 137, 14, 20, 76, 206, 204, 141, 74, 139, 201, 17,
+        78, 19, 21, 138, 143, 81, 211, 75, 23, 205, 142, 18, 79, 85, 215, 144, 80, 210, 148, 22,
+        82, 208, 145, 86, 214, 84, 149, 212, 209, 147, 83, 146, 213, 87, 151, 150,
     ),
     (
         0, 64, 128, 192, 4, 68, 132, 196, 65, 195, 69, 199, 66, 194, 70, 198, 193, 67, 129, 131,
-        1, 3, 197, 71, 5, 133, 7, 135, 130, 2, 6, 134, 8, 72, 136, 200, 73, 203, 12, 76,
-        140, 204, 16, 80, 144, 208, 20, 84, 148, 212, 74, 202, 77, 207, 81, 211, 9, 11, 137, 139,
-        85, 215, 201, 75, 10, 138, 78, 206, 13, 15, 82, 210, 141, 143, 86, 214, 17, 205, 79, 147,
-        19, 145, 209, 83, 14, 21, 213, 87, 23, 151, 149, 142, 18, 146, 22, 150,
+        1, 3, 197, 71, 5, 133, 7, 135, 130, 2, 6, 134, 8, 72, 136, 200, 12, 76, 140, 204,
+        73, 203, 77, 207, 16, 80, 144, 208, 20, 84, 148, 212, 74, 202, 78, 206, 81, 211, 9, 11,
+        137, 139, 85, 215, 201, 75, 13, 15, 141, 143, 205, 79, 10, 82, 210, 138, 14, 86, 214, 142,
+        209, 83, 17, 147, 213, 87, 19, 145, 21, 151, 23, 149, 18, 146, 22, 150,
     ),
     (
         128, 132, 129, 131, 65, 195, 133, 135, 69, 199, 0, 64, 66, 194, 192, 130, 4, 198, 68, 70,
-        196, 134, 193, 1, 3, 67, 197, 71, 5, 7, 2, 6, 136, 73, 203, 137, 139, 140, 8, 72,
-        200, 74, 144, 138, 148, 141, 143, 11, 9, 202, 147, 75, 145, 12, 77, 207, 151, 149, 10, 142,
-        16, 201, 81, 211, 204, 78, 146, 15, 13, 20, 85, 215, 76, 150, 208, 82, 79, 19, 206, 80,
-        210, 84, 14, 17, 212, 86, 214, 205, 83, 23, 209, 18, 87, 21, 213, 22,
+        196, 134, 193, 1, 3, 67, 197, 71, 5, 7, 2, 6, 136, 140, 73, 203, 137, 139, 141, 143,
+        8, 77, 207, 72, 12, 200, 74, 144, 11, 138, 148, 142, 204, 78, 9, 76, 202, 15, 206, 147,
+        10, 75, 13, 145, 151, 81, 211, 201, 149, 14, 16, 79, 205, 85, 215, 146, 20, 208, 82, 210,
+        19, 80, 150, 214, 86, 212, 17, 23, 84, 18, 83, 209, 213, 87, 21, 22,
     ),
     (
         0, 128, 4, 132, 129, 3, 1, 65, 131, 195, 133, 7, 5, 69, 135, 199, 194, 130, 66, 64,
-        2, 192, 198, 70, 68, 196, 6, 134, 67, 193, 71, 197, 8, 136, 203, 11, 73, 137, 9, 139,
-        12, 72, 200, 140, 10, 138, 16, 144, 15, 141, 13, 20, 148, 19, 145, 143, 14, 202, 142, 74,
-        17, 149, 23, 147, 18, 146, 207, 21, 77, 151, 201, 75, 211, 22, 150, 81, 76, 215, 204, 85,
-        78, 80, 208, 206, 82, 84, 212, 210, 86, 205, 79, 214, 209, 83, 213, 87,
+        2, 192, 198, 70, 68, 196, 6, 134, 67, 193, 71, 197, 8, 136, 12, 140, 11, 137, 203, 73,
+        9, 15, 141, 10, 139, 13, 138, 143, 200, 72, 207, 77, 14, 142, 16, 144, 76, 204, 20, 148,
+        19, 145, 74, 202, 149, 23, 17, 206, 78, 18, 147, 75, 146, 201, 21, 211, 81, 151, 22, 150,
+        205, 79, 215, 85, 80, 208, 82, 210, 84, 212, 86, 214, 209, 83, 213, 87,
     ),
     (
         0, 4, 1, 3, 65, 195, 5, 7, 69, 199, 128, 64, 2, 66, 192, 194, 132, 70, 68, 6,
-        196, 198, 129, 67, 193, 131, 71, 133, 197, 135, 130, 134, 8, 73, 203, 9, 11, 12, 72, 200,
-        202, 136, 10, 16, 13, 15, 20, 137, 201, 17, 74, 139, 19, 14, 21, 77, 207, 140, 23, 138,
-        76, 206, 144, 75, 18, 81, 211, 141, 148, 204, 22, 85, 215, 205, 80, 210, 143, 145, 208, 78,
-        212, 82, 214, 84, 142, 79, 209, 86, 149, 147, 83, 213, 87, 146, 151, 150,
+        196, 198, 129, 67, 193, 131, 71, 133, 197, 135, 130, 134, 8, 12, 73, 203, 9, 11, 13, 15,
+        77, 207, 136, 200, 72, 202, 10, 140, 16, 137, 14, 20, 76, 206, 204, 141, 74, 139, 201, 17,
+        78, 19, 21, 138, 143, 81, 211, 75, 23, 205, 142, 18, 79, 85, 215, 144, 80, 210, 148, 22,
+        82, 208, 145, 86, 214, 84, 149, 212, 209, 147, 83, 146, 213, 87, 151, 150,
     ),
 )
 
@@ -197,8 +197,8 @@
 
 
 TILE = 512
-EXTRA = 2
-HOOKS = (1, 4, 6, 8, 10, 13, 15)
+EXTRA = 4
+HOOKS = (2, 4, 7, 10, 12, 15)
 
 
 def panels_kernel(
@@ -606,23 +606,23 @@
 
 def update_kernel(m, ar, wh, wl, top, out):
     i = pl.program_id(0)
-    rows = pl.ds(pl.multiple_of(i * 256, 256), 256)
+    rows = pl.ds(pl.multiple_of(i * 512, 512), 512)
     total = m[rows]
     left = split(jnp.concatenate([ar[s, rows] for s in range(4)], axis=1))
     out[...] = total - product(left, (wh[...], wl[...]))
 
     @pl.when((i == 0) & (lax.axis_index("prow") < 4))
     def _():
-        out[...] = top[...]
+        out[0:256, :] = top[...]
 
 
 def shards(matrix):
     return pl.pallas_call(
         update_kernel,
-        grid=(8,),
+        grid=(4,),
         out_shape=jax.ShapeDtypeStruct((2048, 1024), F32),
         in_specs=[pl.BlockSpec(memory_space=pltpu.VMEM)] * 5,
-        out_specs=pl.BlockSpec((256, 1024), lambda i: (i, 0)),
+        out_specs=pl.BlockSpec((512, 1024), lambda i: (i, 0)),
         compiler_params=pltpu.CompilerParams(vmem_limit_bytes=20 << 20),
         name="update",
     )(*panels(matrix))

time: 137 us -> 132 us (0.964)
  Pallas kernels: 136 us -> 132 us
    pallas_call x1, Pallas kernels: 121 us -> 117 us  [panels(): pl.pallas_call(panels_kernel, out_shape=[jax.ShapeDtypeStruct((2048, 1024...]
where the time goes in v4:
time: 132 us
  Pallas kernels  132 us (100%)
    pallas_call x1, Pallas kernels, panels(): pl.pallas_call(panels_kernel, out_shape=[jax.ShapeDtypeStruct((2048, 1024...  117 us
    pallas_call x1, Pallas kernels, shards(): pl.pallas_call(update_kernel, grid=(4,), out_shape=jax.ShapeDtypeStruct((...  15 us

profile of v4, /device:TPU:22, one launch (start us, length us, event | category | flops | bytes accessed | tf_op | source)
XLA Modules:
  0.0 131.9 jit_solution(7133142184821363274)
XLA Ops:
  0.0 116.9 %panels.1 = (f32[2048,1024]{1,0:T(8,128)S(1)}, f32[4,2048,256]{2,1,0:T(8,128)S(1)}, bf16[1024,1024]{1,0:T(8,128)(2,1)S(1)}, bf16[1024,1024]{1,0:T(8,128)(2,1)S(1)}, f32[256,1024]{1,0:T(8,128)S(1)}) custom-call(f32[2048,1024]{1,0:T(8,128)} %k_ref.1), custom_call_target="tpu_custom_call" | custom-call | tf_op jit(solution)/shard_map/panels/pallas_call | solution.py:582
  116.9 15.0 %update.1 = f32[2048,1024]{1,0:T(8,128)} custom-call(f32[2048,1024]{1,0:T(8,128)S(1)} %get-tuple-element.10.m, f32[4,2048,256]{2,1,0:T(8,128)S(1)} %get-tuple-element.11.ar, bf16[1024,1024]{1,0:T(8,128)(2,1)S(1)} %get-tuple-element.12.wh, bf16[1024,1024]{1,0:T(8,128)(2,1)S(1)} %get-tuple-element.13.wl, f32[256,1024]{1,0:T(8,128)S(1)} %get-tuple-element.14.top), custom_call_target="tpu_custom_call" | custom-call | tf_op jit(solution)/shard_map/update/pallas_call | solution.py:620
